TPU v7x, 256 devices: a whole 4x4x8 slice. The times are simulated.
256 devices in a mesh: sec: 4 (over z_lo, core), seq: 64 (over y, x, z_hi).
Axes of the slice: x: 4, y: 4, z: 8 (z_hi: 4, z_lo: 2; z = z_hi * 2 + z_lo), core: 2. Of those that a mesh axis runs over, the one named last changes fastest.
Arguments:
- queries: bfloat16 [4, 6144, 4096], P('sec', 'seq'), may hold values from -6 to 6
- keys: bfloat16 [4, 6144, 4096], P('sec', 'seq'), may hold values from -6 to 6
- values: bfloat16 [4, 6144, 4096], P('sec', 'seq'), may hold values from -6 to 6
- query_gain: float32 [4096], replicated, may hold values from 0.1 to 1.9
- key_gain: float32 [4096], replicated, may hold values from 0.1 to 1.9
- noisy: float32 [4, 6144, 64], P('sec', 'seq'), may hold values from -6 to 6
- head_weight: bfloat16 [4096, 64], replicated, may hold values from -3 to 3
- conv_in_weight: bfloat16 [3, 3, 3, 16, 384], replicated, may hold values from -0.3125 to 0.3125
- conv_in_bias: float32 [384], replicated, may hold values from -3 to 3
- vae_gain: float32 [384], replicated, may hold values from 0.1 to 1.9
- conv_weight: bfloat16 [3, 3, 3, 384, 384], replicated, may hold values from -0.0625 to 0.0625
Outputs:
- latents: float32 [4, 6144, 64], P('sec', 'seq')
- decoded: bfloat16 [4, 8, 128, 24, 384], P(None, 'sec', 'seq')
All inputs are finite; a program needn't handle non-finite values.
Results may differ from a plain program's by a relative error of at most 0.013.
The roundings to bfloat16 on the way count: a program that leaves them out, or rounds other values in their place, can miss the bound.
Values may be sent and summed in bfloat16 or wider, within the bound.
A program may use at most 64 MiB of HBM per device.

v0:
```python
import math

import jax
import jax.numpy as jnp
from jax import lax
from jax.sharding import PartitionSpec as P

HEADS = 32
HEAD_DIM = 128
LAT_CH = 16
SLAB = 2
PCOLS = 12


eps = 1e-06


def passed_along(array, axis, by):
    length = lax.axis_size(axis)
    pairs = [(i, i + by) for i in range(length) if 0 <= i + by < length]
    return lax.ppermute(array, axis, pairs)


def padded_2(array, sides, width):
    for axis, dim in sides:
        size, length = (lax.axis_size(axis), array.shape[dim])
        up = [(i, (i + 1) % size) for i in range(size - 1)]
        down = [(j, i) for i, j in up]
        last = lax.slice_in_dim(array, length - width, length, axis=dim)
        leading = lax.slice_in_dim(array, 0, width, axis=dim)
        before = lax.ppermute(last, axis, up)
        after = lax.ppermute(leading, axis, down)
        array = jnp.concatenate([before, array, after], axis=dim)
    return array


def rms_scale(values_in, gain):
    floats = values_in.astype(jnp.float32)
    meansq = jnp.mean(floats * floats, axis=-1, keepdims=True)
    return floats * lax.rsqrt(meansq + eps) * gain


def conv_block(extended, weight, frames_out, rows_out):
    col_count = extended.shape[3]
    padded = jnp.pad(extended, ((0, 0), (0, 0), (0, 0), (1, 1), (0, 0)))
    pieces = []
    for time_off in range(3):
        for row_off in range(3):
            for col_off in range(3):
                pieces.append(
                    padded[
                        :,
                        time_off : time_off + frames_out,
                        row_off : row_off + rows_out,
                        col_off : col_off + col_count,
                        :,
                    ]
                )
    flat_weight = weight.reshape(-1, weight.shape[-1])
    return jnp.dot(jnp.concatenate(pieces, -1), flat_weight, preferred_element_type=jnp.float32)


def full_attention(query_rows, key_rows, value_rows):
    query_count = query_rows.shape[0]
    block_rows = math.gcd(query_count, 512)
    factor = 1.0 / math.sqrt(query_rows.shape[-1])

    def one_block(query_block):
        scores = (
            jnp.einsum("qgd,kgd->gqk", query_block, key_rows, preferred_element_type=jnp.float32)
            * factor
        )
        maxima = jnp.max(scores, axis=-1)
        exp_scores = jnp.exp(scores - maxima[..., None])
        totals = jnp.sum(exp_scores, axis=-1)
        weights = exp_scores.astype(jnp.bfloat16)
        summed = jnp.einsum("gqk,kgd->qgd", weights, value_rows, preferred_element_type=jnp.float32)
        return (summed / jnp.transpose(totals)[..., None]).astype(jnp.bfloat16)

    blocks = query_rows.reshape(
        query_count // block_rows, block_rows, query_rows.shape[1], query_rows.shape[2]
    )
    attended = lax.map(one_block, blocks)
    return attended.reshape(query_count, query_rows.shape[1], query_rows.shape[2])


def shards(
    queries,
    keys,
    values,
    query_gain,
    key_gain,
    noisy,
    head_weight,
    conv_in_weight,
    conv_in_bias,
    vae_gain,
    conv_weight,
):
    seq_count = lax.axis_size("seq")
    sec_count = lax.axis_size("sec")
    tok_rows = queries.shape[1]
    channels = queries.shape[2]
    group = max(HEADS // seq_count, 1)
    split = max(seq_count // HEADS, 1)
    head_groups = HEADS // group
    group_cols = group * HEAD_DIM
    part_rows = tok_rows // split
    q_norm = rms_scale(queries[0], query_gain).astype(jnp.bfloat16)
    k_norm = rms_scale(keys[0], key_gain).astype(jnp.bfloat16)
    v_local = values[0]

    def by_heads(array):
        return array.reshape(tok_rows, head_groups, group_cols).transpose(1, 0, 2)

    def duplicated(array):
        return jnp.repeat(by_heads(array), split, axis=0)

    got_q, got_k, got_v = (
        lax.all_to_all(
            by_heads(q_norm).reshape(seq_count, part_rows, group_cols),
            "seq",
            split_axis=0,
            concat_axis=1,
            tiled=True,
        ),
        lax.all_to_all(duplicated(k_norm), "seq", split_axis=0, concat_axis=1, tiled=True),
        lax.all_to_all(duplicated(v_local), "seq", split_axis=0, concat_axis=1, tiled=True),
    )
    got_q = got_q.reshape(-1, group, HEAD_DIM)
    got_k = got_k.reshape(-1, group, HEAD_DIM)
    got_v = got_v.reshape(-1, group, HEAD_DIM)
    attended = full_attention(got_q, got_k, got_v)
    returned = lax.all_to_all(
        attended.reshape(seq_count, part_rows, group_cols),
        "seq",
        split_axis=0,
        concat_axis=0,
        tiled=True,
    )
    tokens_out = (
        returned.reshape(head_groups, split, part_rows, group_cols)
        .transpose(1, 2, 0, 3)
        .reshape(tok_rows, channels)
    )
    velocity = jnp.dot(tokens_out, head_weight, preferred_element_type=jnp.float32)
    latents = noisy[0] + velocity
    frames = SLAB * sec_count
    col_count = 2 * PCOLS
    video = latents.astype(jnp.bfloat16).reshape(frames, PCOLS, 2, 2, LAT_CH)
    video = video.transpose(0, 2, 1, 3, 4).reshape(sec_count, SLAB, 2, col_count, LAT_CH)
    slab_in = lax.all_to_all(video, "sec", split_axis=0, concat_axis=0, tiled=True)
    prev_tail = passed_along(slab_in, "sec", 1)
    stacked = jnp.concatenate([prev_tail, slab_in], 1)
    reach = 1
    padded_in = padded_2(stacked, (("seq", 2),), reach)
    hidden = (conv_block(padded_in, conv_in_weight, SLAB, 2) + conv_in_bias).astype(jnp.bfloat16)
    act = jax.nn.silu(rms_scale(hidden, vae_gain)).astype(jnp.bfloat16)
    act_prev = passed_along(act, "sec", 1)
    act_padded = padded_2(jnp.concatenate([act_prev, act], 1), (("seq", 2),), 1)
    branch_out = conv_block(act_padded, conv_weight, SLAB, 2)
    decoded = (hidden.astype(jnp.float32) + branch_out).astype(jnp.bfloat16)
    return (latents[None], decoded)


def solution(mesh):
    placed = (
        P("sec", "seq", None),
        P("sec", "seq", None),
        P("sec", "seq", None),
        P(),
        P(),
        P("sec", "seq", None),
        P(),
        P(),
        P(),
        P(),
        P(),
    )
    return jax.shard_map(
        shards,
        mesh=mesh,
        in_specs=placed,
        out_specs=(P("sec", "seq", None), P(None, "sec", "seq", None, None)),
        check_vma=False,
    )
```

profile of v0, /device:TPU:9, one launch (start us, length us, event | category | flops | bytes accessed | tf_op | source)
XLA Modules:
  0.0 284.1 jit_solution(5235150968896598590)
XLA Ops:
  0.7 1.5 fusion.37
  2.1 1.3 convert_bitcast_fusion.1
  3.5 0.3 copy.52
  3.7 2.6 fusion.45
  6.4 14.1 %all-to-all-start = ((bf16[64,48,128]{2,1,0:T(8,128)(2,1)}), bf16[64,48,128]{2,1,0:T(8,128)(2,1)S(1)}, u32[]{:S(2)}, u32[]{:S(2)}) async-start(bf16[64,48,128]{2,1,0:T(8,128)(2,1)} %bitcast.10), calls=%async_computation | async-start | bytes 1572864 | tf_op jit(solution)/shard_map/all_to_all | solution.py:120
  20.5 0.2 copy.54
  20.7 0.3 copy.41
  21.0 21.7 %all-to-all-done = bf16[64,48,128]{2,1,0:T(8,128)(2,1)S(1)} async-done(((bf16[64,48,128]{2,1,0:T(8,128)(2,1)}), bf16[64,48,128]{2,1,0:T(8,128)(2,1)S(1)}, u32[]{:S(2)}, u32[]{:S(2)}) %all-to-all-start) | async-done | bytes 786464 | tf_op jit(solution)/shard_map/all_to_all | solution.py:120
  42.7 1.4 broadcast_in_dim.26
  44.1 8.0 %all-to-all-start.2 = ((bf16[64,96,128]{2,1,0:T(8,128)(2,1)}), bf16[64,96,128]{2,1,0:T(8,128)(2,1)}, u32[]{:S(2)}, u32[]{:S(2)}) async-start(bf16[64,96,128]{2,1,0:T(8,128)(2,1)} %bitcast.18), calls=%async_computation.2 | async-start | bytes 3145728 | tf_op jit(solution)/shard_map/all_to_all | solution.py:128
  52.2 0.3 copy.53
  52.5 0.3 fusion.38
  52.7 0.2 fusion.40
  53.0 0.3 copy.40
  53.3 39.0 %all-to-all-done.2 = bf16[64,96,128]{2,1,0:T(8,128)(2,1)} async-done(((bf16[64,96,128]{2,1,0:T(8,128)(2,1)}), bf16[64,96,128]{2,1,0:T(8,128)(2,1)}, u32[]{:S(2)}, u32[]{:S(2)}) %all-to-all-start.2) | async-done | bytes 1572896 | tf_op jit(solution)/shard_map/all_to_all | solution.py:128
  92.3 1.4 broadcast_in_dim.14
  93.7 6.5 %all-to-all-start.1 = ((bf16[64,96,128]{2,1,0:T(8,128)(2,1)}), bf16[64,96,128]{2,1,0:T(8,128)(2,1)S(1)}, u32[]{:S(2)}, u32[]{:S(2)}) async-start(bf16[64,96,128]{2,1,0:T(8,128)(2,1)} %bitcast.116), calls=%async_computation.1 | async-start | bytes 3145728 | tf_op jit(solution)/shard_map/all_to_all | solution.py:127
  100.2 34.1 %all-to-all-done.1 = bf16[64,96,128]{2,1,0:T(8,128)(2,1)S(1)} async-done(((bf16[64,96,128]{2,1,0:T(8,128)(2,1)}), bf16[64,96,128]{2,1,0:T(8,128)(2,1)S(1)}, u32[]{:S(2)}, u32[]{:S(2)}) %all-to-all-start.1) | async-done | bytes 1572896 | tf_op jit(solution)/shard_map/all_to_all | solution.py:127
  134.3 49.7 %while.10 = (s32[]{:T(128)}, bf16[6,512,1,128]{3,1,2,0:T(8,128)(2,1)}, bf16[6,512,1,128]{3,1,2,0:T(8,128)(2,1)S(1)}, bf16[6144,1,128]{2,0,1:T(8,128)(2,1)S(1)}, bf16[6144,1,128]{2,0,1:T(8,128)(2,1)}, /*index=5*/s32[]{:T(128)}) while((s32[]{:T(128)}, bf16[6,512,1,128]{3,1,2,0:T(8,128)(2,1)}, bf16[6,512,1,128]{3,1,2,0:T(8,128)(2,1)S(1)}, ...), condition=%wide.region_5.6_spmd, body=%wide.region_2.5_spmd.sunk | while | flops 1635908608 | bytes 41166932 | solution.py:83
  134.3 1.9 multiply_reduce_fusion.3
  136.2 2.2 fusion.75
  138.3 4.2 %fusion.76 = bf16[6,512,1,128]{3,1,2,0:T(8,128)(2,1)} fusion(bf16[6,512,1,128]{3,1,2,0:T(8,128)(2,1)} %get-tuple-element.143, s32[]{:T(128)S(6)} %copy.70, bf16[6144,1,128]{2,0,1:T(8,128)(2,1)} %get-tuple-element.152, f32[512,6144]{1,0:T(8,128)S(1)} %get-tuple-element.134, f32[512]{0:T(512)S(1)} %get-tuple-element.135, f32[512]{0:T(512)S(1)} %fusion.75), kind=kOutput, calls=%fused_computation.12.clone.1 | convolution fusion | flops 814874624 | bytes 14290948 | tf_op jit(solution)/shard_map/while/body/eval_jaxpr/gqk,kgd->qgd/dot_general | solution.py:77
  142.6 1.9 multiply_reduce_fusion.3
  144.4 2.2 fusion.75
  146.6 4.2 %fusion.76 = bf16[6,512,1,128]{3,1,2,0:T(8,128)(2,1)} fusion(bf16[6,512,1,128]{3,1,2,0:T(8,128)(2,1)} %get-tuple-element.143, s32[]{:T(128)S(6)} %copy.70, bf16[6144,1,128]{2,0,1:T(8,128)(2,1)} %get-tuple-element.152, f32[512,6144]{1,0:T(8,128)S(1)} %get-tuple-element.134, f32[512]{0:T(512)S(1)} %get-tuple-element.135, f32[512]{0:T(512)S(1)} %fusion.75), kind=kOutput, calls=%fused_computation.12.clone.1 | convolution fusion | flops 814874624 | bytes 14290948 | tf_op jit(solution)/shard_map/while/body/eval_jaxpr/gqk,kgd->qgd/dot_general | solution.py:77
  150.8 1.9 multiply_reduce_fusion.3
  152.7 2.2 fusion.75
  154.9 4.2 %fusion.76 = bf16[6,512,1,128]{3,1,2,0:T(8,128)(2,1)} fusion(bf16[6,512,1,128]{3,1,2,0:T(8,128)(2,1)} %get-tuple-element.143, s32[]{:T(128)S(6)} %copy.70, bf16[6144,1,128]{2,0,1:T(8,128)(2,1)} %get-tuple-element.152, f32[512,6144]{1,0:T(8,128)S(1)} %get-tuple-element.134, f32[512]{0:T(512)S(1)} %get-tuple-element.135, f32[512]{0:T(512)S(1)} %fusion.75), kind=kOutput, calls=%fused_computation.12.clone.1 | convolution fusion | flops 814874624 | bytes 14290948 | tf_op jit(solution)/shard_map/while/body/eval_jaxpr/gqk,kgd->qgd/dot_general | solution.py:77
  159.1 1.9 multiply_reduce_fusion.3
  161.0 2.2 fusion.75
  163.2 4.2 %fusion.76 = bf16[6,512,1,128]{3,1,2,0:T(8,128)(2,1)} fusion(bf16[6,512,1,128]{3,1,2,0:T(8,128)(2,1)} %get-tuple-element.143, s32[]{:T(128)S(6)} %copy.70, bf16[6144,1,128]{2,0,1:T(8,128)(2,1)} %get-tuple-element.152, f32[512,6144]{1,0:T(8,128)S(1)} %get-tuple-element.134, f32[512]{0:T(512)S(1)} %get-tuple-element.135, f32[512]{0:T(512)S(1)} %fusion.75), kind=kOutput, calls=%fused_computation.12.clone.1 | convolution fusion | flops 814874624 | bytes 14290948 | tf_op jit(solution)/shard_map/while/body/eval_jaxpr/gqk,kgd->qgd/dot_general | solution.py:77
  167.4 1.9 multiply_reduce_fusion.3
  169.3 2.2 fusion.75
  171.4 4.2 %fusion.76 = bf16[6,512,1,128]{3,1,2,0:T(8,128)(2,1)} fusion(bf16[6,512,1,128]{3,1,2,0:T(8,128)(2,1)} %get-tuple-element.143, s32[]{:T(128)S(6)} %copy.70, bf16[6144,1,128]{2,0,1:T(8,128)(2,1)} %get-tuple-element.152, f32[512,6144]{1,0:T(8,128)S(1)} %get-tuple-element.134, f32[512]{0:T(512)S(1)} %get-tuple-element.135, f32[512]{0:T(512)S(1)} %fusion.75), kind=kOutput, calls=%fused_computation.12.clone.1 | convolution fusion | flops 814874624 | bytes 14290948 | tf_op jit(solution)/shard_map/while/body/eval_jaxpr/gqk,kgd->qgd/dot_general | solution.py:77
  175.7 1.9 multiply_reduce_fusion.3
  177.5 2.2 fusion.75
  179.7 4.2 %fusion.76 = bf16[6,512,1,128]{3,1,2,0:T(8,128)(2,1)} fusion(bf16[6,512,1,128]{3,1,2,0:T(8,128)(2,1)} %get-tuple-element.143, s32[]{:T(128)S(6)} %copy.70, bf16[6144,1,128]{2,0,1:T(8,128)(2,1)} %get-tuple-element.152, f32[512,6144]{1,0:T(8,128)S(1)} %get-tuple-element.134, f32[512]{0:T(512)S(1)} %get-tuple-element.135, f32[512]{0:T(512)S(1)} %fusion.75), kind=kOutput, calls=%fused_computation.12.clone.1 | convolution fusion | flops 814874624 | bytes 14290948 | tf_op jit(solution)/shard_map/while/body/eval_jaxpr/gqk,kgd->qgd/dot_general | solution.py:77
  184.0 23.6 %all_to_all.37 = bf16[64,48,128]{2,1,0:T(8,128)(2,1)S(1)} all-to-all(bf16[64,48,128]{2,1,0:T(8,128)(2,1)} %bitcast.123), channel_id=1, replica_groups=mesh['sec'=4,'seq'=64] {'seq'}, dimensions={0} | all-to-all | bytes 1572864 | tf_op jit(solution)/shard_map/all_to_all | solution.py:134
  207.6 0.3 copy.43
  207.9 1.1 fusion.63
  209.5 12.9 %all_to_all.38 = bf16[4,2,768]{2,1,0:T(2,128)(2,1)S(1)} all-to-all(bf16[4,2,768]{2,1,0:T(2,128)(2,1)S(1)} %reshape.152), channel_id=1, replica_groups=mesh['sec'=4,'seq'=64] {'sec'}, dimensions={0} | all-to-all | bytes 24576 | tf_op jit(solution)/shard_map/all_to_all | solution.py:152
  222.6 2.3 collective-permute-start
  224.9 1.6 collective-permute-done
  226.5 1.9 collective-permute-start.1
  228.5 8.5 %collective-permute-start.2 = (bf16[4,4,1,24,16]{4,3,2,1,0:T(8,128)(2,1)S(1)}, bf16[4,4,1,24,16]{4,3,2,1,0:T(8,128)(2,1)S(1)}, u32[]{:S(2)}, u32[]{:S(2)}) collective-permute-start(bf16[4,4,1,24,16]{4,3,2,1,0:T(8,128)(2,1)S(1)} %get-tuple-element.93), channel_id=1, source_target_pairs={{1,0},{2,1},{3,2},{4,3},{5,4},{6,5},{7,6},{8,7},{9,8},{10,9},{11,1... | collective-permute-start | bytes 36872 | tf_op jit(solution)/shard_map/ppermute | solution.py:32
  237.0 0.7 pad_maximum_fusion.3
  237.6 1.6 collective-permute-done.1
  239.2 0.2 collective-permute-done.2
  239.4 0.2 select_maximum_fusion.2
  239.7 0.3 fusion.60
  240.2 2.2 concatenate.42
  242.5 1.4 multiply_reduce_fusion.1
  243.9 0.2 multiply_convert_fusion
  244.2 4.6 %collective-permute-start.3 = (bf16[4,2,2,24,384]{4,3,2,1,0:T(8,128)(2,1)S(1)}, bf16[4,2,2,24,384]{4,3,2,1,0:T(8,128)(2,1)S(1)}, u32[]{:S(2)}, u32[]{:S(2)}) collective-permute-start(bf16[4,2,2,24,384]{4,3,2,1,0:T(8,128)(2,1)S(1)} %multiply_convert_fusion), channel_id=1, source_target_pairs={{0,64},{64,128},{128,192},{1,65},{65,129},{129,193},{2,66},{66,130... | collective-permute-start | bytes 884744 | tf_op jit(solution)/shard_map/ppermute | solution.py:21
  248.8 7.3 %collective-permute-done.3 = bf16[4,2,2,24,384]{4,3,2,1,0:T(8,128)(2,1)S(1)} collective-permute-done((bf16[4,2,2,24,384]{4,3,2,1,0:T(8,128)(2,1)S(1)}, bf16[4,2,2,24,384]{4,3,2,1,0:T(8,128)(2,1)S(1)}, u32[]{:S(2)}, u32[]{:S(2)}) %collective-permute-start.3) | collective-permute-done | bytes 294944 | tf_op jit(solution)/shard_map/ppermute | solution.py:21
  256.2 1.9 collective-permute-start.4
  258.1 9.5 %collective-permute-start.5 = (bf16[4,4,1,24,384]{4,3,2,1,0:T(8,128)(2,1)S(1)}, bf16[4,4,1,24,384]{4,3,2,1,0:T(8,128)(2,1)S(1)}, u32[]{:S(2)}, u32[]{:S(2)}) collective-permute-start(bf16[4,4,1,24,384]{4,3,2,1,0:T(8,128)(2,1)S(1)} %get-tuple-element.65), channel_id=1, source_target_pairs={{1,0},{2,1},{3,2},{4,3},{5,4},{6,5},{7,6},{8,7},{9,8},{10,9},{11,1... | collective-permute-start | bytes 884744 | tf_op jit(solution)/shard_map/ppermute | solution.py:32
  267.6 2.1 collective-permute-done.4
  269.7 4.5 %collective-permute-done.5 = bf16[4,4,1,24,384]{4,3,2,1,0:T(8,128)(2,1)S(1)} collective-permute-done((bf16[4,4,1,24,384]{4,3,2,1,0:T(8,128)(2,1)S(1)}, bf16[4,4,1,24,384]{4,3,2,1,0:T(8,128)(2,1)S(1)}, u32[]{:S(2)}, u32[]{:S(2)}) %collective-permute-start.5) | collective-permute-done | bytes 294944 | tf_op jit(solution)/shard_map/ppermute | solution.py:32
  274.2 0.8 select_maximum_fusion
  275.1 0.3 pad_maximum_fusion
  277.0 0.3 constant_dynamic-update-slice_fusion
  277.7 1.3 slice-done.1
  278.9 5.1 %fusion.48 = bf16[4,2,2,24,384]{4,3,2,1,0:T(8,128)(2,1)} fusion(f32[4,2,2,24,384]{4,3,2,1,0:T(8,128)S(1)} %get-tuple-element.97, bf16[4,2,2,24,10368]{4,3,2,1,0:T(8,128)(2,1)S(1)} %slice_dynamic-update-slice_fusion, bf16[10368,384,1,1,1]{1,0,4,3,2:T(8,128)(2,1)S(1)} %bitcast.134), kind=kOutput, calls=%fused_computation.43 | convolution fusion | flops 3057942528 | bytes 16809984 | tf_op jit(solution)/shard_map/dot_general | solution.py:60
  (60 shorter events, 3.2 us)
Async XLA Ops:
  0.6 207.2 %copy-start = (bf16[4096,64]{0,1:T(8,128)(2,1)S(1)}, bf16[4096,64]{0,1:T(8,128)(2,1)}, u32[]{:S(2)}) copy-start(bf16[4096,64]{0,1:T(8,128)(2,1)} %param.19) | copy-start | bytes 1572868
  0.6 19.9 %copy-start.2 = (bf16[1,96,4096]{2,1,0:T(8,128)(2,1)S(1)}, bf16[1,96,4096]{2,1,0:T(8,128)(2,1)}, u32[]{:S(2)}) copy-start(bf16[1,96,4096]{2,1,0:T(8,128)(2,1)} %param.15) | copy-start | bytes 2359300
  3.4 48.6 %copy-start.1 = (bf16[1,96,4096]{2,1,0:T(8,128)(2,1)S(1)}, bf16[1,96,4096]{2,1,0:T(8,128)(2,1)}, u32[]{:S(2)}) copy-start(bf16[1,96,4096]{2,1,0:T(8,128)(2,1)} %param.14) | copy-start | bytes 2359300
  6.4 46.4 %copy-start.3 = (f32[4096]{0:T(1024)S(1)}, f32[4096]{0:T(1024)}, u32[]{:S(2)}) copy-start(f32[4096]{0:T(1024)} %param.17) | copy-start | bytes 49156
  6.4 36.3 %all-to-all-start = ((bf16[64,48,128]{2,1,0:T(8,128)(2,1)}), bf16[64,48,128]{2,1,0:T(8,128)(2,1)S(1)}, u32[]{:S(2)}, u32[]{:S(2)}) async-start(bf16[64,48,128]{2,1,0:T(8,128)(2,1)} %bitcast.10), calls=%async_computation | async-start | bytes 1572864 | tf_op jit(solution)/shard_map/all_to_all | solution.py:120
  44.1 48.2 %all-to-all-start.2 = ((bf16[64,96,128]{2,1,0:T(8,128)(2,1)}), bf16[64,96,128]{2,1,0:T(8,128)(2,1)}, u32[]{:S(2)}, u32[]{:S(2)}) async-start(bf16[64,96,128]{2,1,0:T(8,128)(2,1)} %bitcast.18), calls=%async_computation.2 | async-start | bytes 3145728 | tf_op jit(solution)/shard_map/all_to_all | solution.py:128
  93.7 40.6 %all-to-all-start.1 = ((bf16[64,96,128]{2,1,0:T(8,128)(2,1)}), bf16[64,96,128]{2,1,0:T(8,128)(2,1)S(1)}, u32[]{:S(2)}, u32[]{:S(2)}) async-start(bf16[64,96,128]{2,1,0:T(8,128)(2,1)} %bitcast.116), calls=%async_computation.1 | async-start | bytes 3145728 | tf_op jit(solution)/shard_map/all_to_all | solution.py:127
  134.3 73.6 %copy-start.6 = (f32[1,96,64]{1,2,0:T(8,128)S(1)}, f32[1,96,64]{1,2,0:T(8,128)}, u32[]{:S(2)}) copy-start(f32[1,96,64]{1,2,0:T(8,128)} %param.18) | copy-start | bytes 73732
  184.0 58.5 %copy-start.5 = (f32[384]{0:T(512)S(1)}, f32[384]{0:T(512)}, u32[]{:S(2)}) copy-start(f32[384]{0:T(512)} %param.21) | copy-start | bytes 4612
  207.6 36.4 %copy-start.4 = (f32[384]{0:T(512)S(1)}, f32[384]{0:T(512)}, u32[]{:S(2)}) copy-start(f32[384]{0:T(512)} %param.22) | copy-start | bytes 4612
  222.6 3.9 %collective-permute-start = (bf16[4,2,2,24,16]{4,3,2,1,0:T(8,128)(2,1)S(1)}, bf16[4,2,2,24,16]{4,3,2,1,0:T(8,128)(2,1)S(1)}, u32[]{:S(2)}, u32[]{:S(2)}) collective-permute-start(bf16[4,2,2,24,16]{4,3,2,1,0:T(8,128)(2,1)S(1)} %copy.47), channel_id=1, source_target_pairs={{0,64},{64,128},{128,192},{1,65},{65,129},{129,193},{2,66},{66,130... | collective-permute-start | bytes 36872 | tf_op jit(solution)/shard_map/ppermute | solution.py:21
  226.5 12.7 %collective-permute-start.1 = (bf16[4,4,1,24,16]{4,3,2,1,0:T(8,128)(2,1)S(1)}, bf16[4,4,1,24,16]{4,3,2,1,0:T(8,128)(2,1)S(1)}, u32[]{:S(2)}, u32[]{:S(2)}) collective-permute-start(bf16[4,4,1,24,16]{4,3,2,1,0:T(8,128)(2,1)S(1)} %get-tuple-element.92), channel_id=1, source_target_pairs={{0,1},{1,2},{2,3},{3,4},{4,5},{5,6},{6,7},{7,8},{8,9},{9,10},{10,1... | collective-permute-start | bytes 36872 | tf_op jit(solution)/shard_map/ppermute | solution.py:31
  228.5 11.0 %collective-permute-start.2 = (bf16[4,4,1,24,16]{4,3,2,1,0:T(8,128)(2,1)S(1)}, bf16[4,4,1,24,16]{4,3,2,1,0:T(8,128)(2,1)S(1)}, u32[]{:S(2)}, u32[]{:S(2)}) collective-permute-start(bf16[4,4,1,24,16]{4,3,2,1,0:T(8,128)(2,1)S(1)} %get-tuple-element.93), channel_id=1, source_target_pairs={{1,0},{2,1},{3,2},{4,3},{5,4},{6,5},{7,6},{8,7},{9,8},{10,9},{11,1... | collective-permute-start | bytes 36872 | tf_op jit(solution)/shard_map/ppermute | solution.py:32
  244.2 11.9 %collective-permute-start.3 = (bf16[4,2,2,24,384]{4,3,2,1,0:T(8,128)(2,1)S(1)}, bf16[4,2,2,24,384]{4,3,2,1,0:T(8,128)(2,1)S(1)}, u32[]{:S(2)}, u32[]{:S(2)}) collective-permute-start(bf16[4,2,2,24,384]{4,3,2,1,0:T(8,128)(2,1)S(1)} %multiply_convert_fusion), channel_id=1, source_target_pairs={{0,64},{64,128},{128,192},{1,65},{65,129},{129,193},{2,66},{66,130... | collective-permute-start | bytes 884744 | tf_op jit(solution)/shard_map/ppermute | solution.py:21
  256.2 13.5 %collective-permute-start.4 = (bf16[4,4,1,24,384]{4,3,2,1,0:T(8,128)(2,1)S(1)}, bf16[4,4,1,24,384]{4,3,2,1,0:T(8,128)(2,1)S(1)}, u32[]{:S(2)}, u32[]{:S(2)}) collective-permute-start(bf16[4,4,1,24,384]{4,3,2,1,0:T(8,128)(2,1)S(1)} %get-tuple-element.64), channel_id=1, source_target_pairs={{0,1},{1,2},{2,3},{3,4},{4,5},{5,6},{6,7},{7,8},{8,9},{9,10},{10,1... | collective-permute-start | bytes 884744 | tf_op jit(solution)/shard_map/ppermute | solution.py:31
  258.1 16.1 %collective-permute-start.5 = (bf16[4,4,1,24,384]{4,3,2,1,0:T(8,128)(2,1)S(1)}, bf16[4,4,1,24,384]{4,3,2,1,0:T(8,128)(2,1)S(1)}, u32[]{:S(2)}, u32[]{:S(2)}) collective-permute-start(bf16[4,4,1,24,384]{4,3,2,1,0:T(8,128)(2,1)S(1)} %get-tuple-element.65), channel_id=1, source_target_pairs={{1,0},{2,1},{3,2},{4,3},{5,4},{6,5},{7,6},{8,7},{9,8},{10,9},{11,1... | collective-permute-start | bytes 884744 | tf_op jit(solution)/shard_map/ppermute | solution.py:32
  275.3 2.3 slice-start
  276.4 2.6 slice-start.1
where the time goes:
time: 285 us; the launch traced here: 284 us
  waiting for transfers between devices  112 us (39%)
  starting transfers between devices  57.3 us (20%)
  matrix products  44.2 us (16%)
  blocking collectives  36.5 us (13%)
  other arithmetic  22 us (8%)
  local copies, waits for them, and re-layouts  11 us (4%)
    all_to_all x1, waiting for transfers between devices, shards(): lax.all_to_all(duplicated(v_local), 'seq', split_axis=0, concat_axis=1, t...  39 us
    all_to_all x1, waiting for transfers between devices, shards(): lax.all_to_all(duplicated(k_norm), 'seq', split_axis=0, concat_axis=1, ti...  34.1 us
    dot_general x6, matrix products, one_block(): jnp.einsum('gqk,kgd->qgd', weights, value_rows, preferred_element_type=jn...  25.3 us
    all_to_all x1, blocking collectives, shards(): lax.all_to_all(attended.reshape(seq_count, part_rows, group_cols), 'seq',...  23.6 us
    all_to_all x1, waiting for transfers between devices, shards(): lax.all_to_all(by_heads(q_norm).reshape(seq_count, part_rows, group_cols)...  21.7 us
    ppermute x2, starting transfers between devices, padded_2(): after = lax.ppermute(leading, axis, down)  18 us
    all_to_all x1, starting transfers between devices, shards(): lax.all_to_all(by_heads(q_norm).reshape(seq_count, part_rows, group_cols)...  14.1 us
    reduce_sum x6, other arithmetic, one_block(): totals = jnp.sum(exp_scores, axis=-1)  13.1 us
  transfers between devices with their start and end apart: 9, of which 9 were waited for; matrix products, arithmetic and copies ran while one was open for 1% of the time, Pallas kernels for 0%

commit v1 on v0

v1 whole, which is shorter than its diff:
```python
import functools
import math

import jax
import jax.numpy as jnp
import numpy as np
from jax import lax
from jax.experimental import pallas as pl
from jax.experimental.pallas import tpu as pltpu
from jax.sharding import PartitionSpec as P

HEADS = 32
HEAD_DIM = 128
ROWS = 96
HALF = ROWS // 2
SEQ = 64
SEC = 4
STEPS = 32
PER_CHUNK = 4
CHUNKS = STEPS // PER_CHUNK
QB = PER_CHUNK * ROWS
N_QB = STEPS // PER_CHUNK
KC = PER_CHUNK * ROWS
PCOLS = 12
RC = SEC * PCOLS
CH = 384
EPS = 1e-06
MESH = pl.DeviceIdType.MESH
NT = (((1,), (1,)), ((), ()))
LOG2E = 1.0 / math.log(2.0)


def offsets(i):
    b, c = lax.rem(lax.div(i, 4), 4), lax.rem(i, 4)
    dy = lax.rem(lax.div(i, 16) + lax.div(c, 2), 2)
    return dy, lax.rem(b + c, 4), c


def place_after(j, i):
    dy, dx, dz = offsets(i)
    y = lax.rem(lax.div(j, 16) + dy, 2)
    x = lax.rem(lax.rem(lax.div(j, 4), 4) + dx, 4)
    z = lax.rem(lax.rem(j, 4) + dz, 4)
    return y * 16 + x * 4 + z


def place_before(h, i):
    dy, dx, dz = offsets(i)
    y = lax.rem(lax.div(h, 16) + 2 - dy, 2)
    x = lax.rem(lax.rem(lax.div(h, 4), 4) + 4 - dx, 4)
    z = lax.rem(lax.rem(h, 4) + 4 - dz, 4)
    return y * 16 + x * 4 + z


def gather_constants():
    rows = np.zeros((3, 4 * RC, 4 * RC), np.float32)
    lanes = np.zeros((3, 128, 256), np.float32)
    for k in range(3):
        for f in range(4):
            for r in range(SEC):
                for c in range(PCOLS):
                    if 0 <= c + k - 1 < PCOLS:
                        rows[k, (f * SEC + r) * PCOLS + c, (r * 4 + f) * PCOLS + c + k - 1] = 1
    for half in range(2):
        for i in range(2):
            for tap, (k, j) in enumerate(((0, 1), (1, 0), (1, 1), (2, 0))):
                for ch in range(16):
                    lanes[k, half * 64 + i * 32 + j * 16 + ch, half * 128 + i * 64 + tap * 16 + ch] = 1
    return rows, lanes.reshape(384, 256)


def kernel(
    q_ref, k_ref, v_ref, qg_ref, kg_ref, noisy_ref, hw_ref, win_ref, bias_ref, vg_ref, w_ref, rowsel_ref, lanesel_ref,
    lat_ref, dec_ref,
    qsrc, kvsrc, qbuf, kvbuf, sibbuf, acc, m_s, l_s, s_a, s_b, obuf, vbuf,
    xsrc, xrecv, xf, lhs, hid, tap, wbig, wconv, w_h, cacc,
    ssq, sskv, ssf, sso, ssx, rq, rkv, rf, ro, rx, lsem,
):
    sec, p = lax.axis_index("sec"), lax.axis_index("seq")
    z_lo, core = lax.div(sec, 2), lax.rem(sec, 2)
    part, place = lax.div(p, 32), lax.rem(p, 32)

    def target(h):
        return (2 * z_lo + 1 - part, h + 32 * core)

    def source(j):
        return (2 * z_lo + part, j + 32 * (1 - core))

    sibling = (2 * z_lo + 1 - core, p)

    def beside(d):
        return lax.rem(p + SEQ + d, SEQ)

    barrier = pltpu.get_barrier_semaphore()

    def greet(i, _):
        pl.semaphore_signal(barrier, inc=1, device_id=target(place_after(place, i)), device_id_type=MESH)
        pl.semaphore_signal(barrier, inc=1, device_id=source(place_before(place, i)), device_id_type=MESH)
        return 0

    lax.fori_loop(0, STEPS, greet, 0)
    pl.semaphore_signal(barrier, inc=1, device_id=sibling, device_id_type=MESH)
    for d in (-1, 0, 1):
        for s in range(1, SEC) if d == 0 else range(SEC):
            pl.semaphore_signal(barrier, inc=1, device_id=(lax.rem(sec + s, SEC), beside(d)), device_id_type=MESH)

    w_copy = pltpu.make_async_copy(w_ref, wconv, lsem.at[0])
    w_copy.start()
    hw_copy = pltpu.make_async_copy(hw_ref.at[pl.ds(pl.multiple_of(place * HEAD_DIM, HEAD_DIM), HEAD_DIM)], w_h, lsem.at[1])
    hw_copy.start()

    def normed(ref, gain_ref, factor, store):
        def some(t, _):
            rows = pl.ds(pl.multiple_of(t * 16, 16), 16)
            x = ref[rows, :].astype(jnp.float32)
            scale = lax.rsqrt(jnp.mean(x * x, axis=-1, keepdims=True) + EPS)
            for h in range(HEADS):
                cols = slice(h * HEAD_DIM, (h + 1) * HEAD_DIM)
                y = x[:, cols] * scale * gain_ref[:, cols]
                store(h, rows, (y if factor is None else y * factor).astype(jnp.bfloat16))
            return 0

        lax.fori_loop(0, ROWS // 16, some, 0)

    def store_q(h, rows, y):
        qsrc[h, rows, :] = y

    def store_k(h, rows, y):
        kvsrc[h, 0, rows, :] = y

    normed(q_ref, qg_ref, LOG2E / math.sqrt(HEAD_DIM), store_q)
    pl.semaphore_wait(barrier, 2 * STEPS + 1 + 3 * SEC - 1)

    def send_q(i, _):
        h = place_after(place, i)
        pltpu.make_async_remote_copy(
            src_ref=qsrc.at[h], dst_ref=qbuf.at[i], send_sem=ssq, recv_sem=rq, device_id=target(h), device_id_type=MESH
        ).start()
        return 0

    lax.fori_loop(0, STEPS, send_q, 0)
    for h in range(HEADS):
        kvsrc[h, 1] = v_ref[:, h * HEAD_DIM : (h + 1) * HEAD_DIM]
    normed(k_ref, kg_ref, None, store_k)

    def send_kv(i, _):
        h = place_after(place, i)
        pltpu.make_async_remote_copy(
            src_ref=kvsrc.at[h],
            dst_ref=kvbuf.at[i],
            send_sem=sskv,
            recv_sem=rkv.at[lax.div(i, PER_CHUNK)],
            device_id=target(h),
            device_id_type=MESH,
        ).start()
        return 0

    lax.fori_loop(0, STEPS, send_kv, 0)

    wbig[...] = jnp.zeros_like(wbig)
    for a in range(3):
        for b in range(3):
            block = win_ref[pl.ds((a * 3 + b) * 48, 48), :]
            for i in range(2):
                for j in range(2):
                    wbig[pl.ds(a * 256 + (b + i) * 64 + j * 16, 48), pl.ds((i * 2 + j) * CH, CH)] = block
    xf[pl.ds(0, 4)] = jnp.zeros((4,) + xf.shape[1:], jnp.bfloat16)
    acc[...] = jnp.zeros_like(acc)
    l_s[...] = jnp.zeros_like(l_s)
    m_s[...] = jnp.full_like(m_s, -1e30)
    hw_copy.wait()
    w_t = w_h[...].astype(jnp.float32).T.astype(jnp.bfloat16)

    def chunk_of(buffer, g):
        return buffer.at[pl.ds(pl.multiple_of(g * PER_CHUNK, PER_CHUNK), PER_CHUNK)]

    def forward(g):
        return pltpu.make_async_remote_copy(
            src_ref=chunk_of(kvbuf, g),
            dst_ref=chunk_of(sibbuf, g),
            send_sem=ssf.at[g],
            recv_sem=rf.at[g],
            device_id=sibling,
            device_id_type=MESH,
        )

    def arrived(buffer, sem):
        pltpu.make_async_copy(buffer, buffer, sem).wait()

    def pass_on(g):
        arrived(chunk_of(kvbuf, g), rkv.at[g])
        forward(g).start()

    def score(g, j, dst):
        q = qbuf[pl.ds(j * PER_CHUNK, PER_CHUNK)].reshape(QB, HEAD_DIM)
        for n, buffer in enumerate((kvbuf, sibbuf)):
            keys = buffer[pl.ds(g * PER_CHUNK, PER_CHUNK), 0].reshape(KC, HEAD_DIM)
            dst[pl.ds(n * KC, KC), :] = lax.dot_general(keys, q, NT, preferred_element_type=jnp.float32)

    def update(j, src, v_t):
        s = src[...]
        m_old = m_s[j]
        m_new = jnp.maximum(m_old, jnp.max(s, axis=0, keepdims=True))
        m_s[j] = m_new
        alpha = jnp.exp2(m_old - m_new)
        e = jnp.exp2(s - m_new[:1])
        l_s[j] = l_s[j] * alpha + jnp.sum(e.reshape(2 * KC // 8, 8, QB), axis=0)
        acc[j] = acc[j] * alpha[:1] + jnp.dot(v_t, e.astype(jnp.bfloat16), preferred_element_type=jnp.float32)

    def give_back(j):
        total = jnp.sum(l_s[j], axis=0, keepdims=True)
        attended = (acc[j] / total).astype(jnp.bfloat16)
        velocity = jnp.dot(w_t, attended, preferred_element_type=jnp.float32).T
        for n in range(PER_CHUNK):
            rows = velocity[n * ROWS : (n + 1) * ROWS]
            i = j * PER_CHUNK + n
            obuf[i] = jnp.concatenate([rows[:HALF], rows[HALF:]], axis=1).astype(jnp.bfloat16)
            pltpu.make_async_remote_copy(
                src_ref=obuf.at[i],
                dst_ref=vbuf.at[i],
                send_sem=sso,
                recv_sem=ro,
                device_id=source(place_before(place, i)),
                device_id_type=MESH,
            ).start()

    arrived(qbuf, rq)
    pass_on(0)

    def chunk(g, _):
        arrived(chunk_of(sibbuf, g), rf.at[g])
        v_t = jnp.concatenate(
            [buffer[pl.ds(g * PER_CHUNK, PER_CHUNK), 1].reshape(KC, HEAD_DIM).T for buffer in (kvbuf, sibbuf)], axis=1
        )
        last = g == CHUNKS - 1
        score(g, 0, s_a)

        def pair(i, _):
            @pl.when(jnp.logical_and(i == N_QB // 2 - 1, jnp.logical_not(last)))
            def _():
                pass_on(g + 1)

            score(g, 2 * i + 1, s_b)
            update(2 * i, s_a, v_t)
            score(g, lax.rem(2 * i + 2, N_QB), s_a)
            update(2 * i + 1, s_b, v_t)

            @pl.when(last)
            def _():
                give_back(2 * i)
                give_back(2 * i + 1)

            return 0

        lax.fori_loop(0, N_QB // 2, pair, 0)
        return 0

    lax.fori_loop(0, CHUNKS, chunk, 0)

    arrived(vbuf, ro)
    velocity = jnp.sum(vbuf[...].astype(jnp.float32), axis=0)
    first = noisy_ref[pl.ds(0, HALF), :] + velocity[:, :64]
    second = noisy_ref[pl.ds(HALF, HALF), :] + velocity[:, 64:]
    lat_ref[pl.ds(0, HALF), :] = first
    lat_ref[pl.ds(HALF, HALF), :] = second
    patches = jnp.concatenate([first, second], axis=1).astype(jnp.bfloat16)
    xsrc[...] = patches
    xrecv[SEC + sec] = patches
    for d in (-1, 0, 1):
        for s in range(1, SEC) if d == 0 else range(SEC):
            pltpu.make_async_remote_copy(
                src_ref=xsrc,
                dst_ref=xrecv.at[(1 - d) * SEC + sec],
                send_sem=ssx,
                recv_sem=rx,
                device_id=(lax.rem(sec + s, SEC), beside(d)),
                device_id_type=MESH,
            ).start()
    arrived(xrecv.at[pl.ds(0, 3 * SEC - 1)], rx)

    for d in range(3):
        got = xrecv[pl.ds(d * SEC, SEC)].reshape(SEC * HALF, 128)
        shifted = [jnp.dot(rowsel_ref[k], got, preferred_element_type=jnp.float32).astype(jnp.bfloat16) for k in range(3)]
        rows = jnp.dot(jnp.concatenate(shifted, axis=1), lanesel_ref[...], preferred_element_type=jnp.float32)
        if d == 0:
            rows = jnp.where(p == 0, 0.0, rows)
        if d == 2:
            rows = jnp.where(p == SEQ - 1, 0.0, rows)
        rows = rows.astype(jnp.bfloat16)
        for f in range(8):
            xf[4 + f, d] = rows[f % 4 * RC : (f % 4 + 1) * RC, f // 4 * 128 : (f // 4 + 1) * 128]
    for l in range(2):
        for f in range(4):
            for a in range(3):
                for n in range(2):
                    lhs[pl.ds((l * 4 + f) * RC, RC), pl.ds(a * 256 + n * 128, 128)] = xf[2 * sec + f + a, l + n]
    row = lax.broadcasted_iota(jnp.int32, (RC, CH), 0)
    is_first = functools.reduce(jnp.logical_or, [row == r * PCOLS for r in range(SEC)])
    is_last = functools.reduce(jnp.logical_or, [row == r * PCOLS + PCOLS - 1 for r in range(SEC)])
    for i in range(2):
        for j in range(2):
            cols = pl.ds((i * 2 + j) * CH, CH)
            hid[:, cols] = jnp.dot(lhs[...], wbig[:, cols], preferred_element_type=jnp.float32) + bias_ref[...]

        def activate(lf, _):
            l, f = lax.div(lf, 4), lax.rem(lf, 4)
            y = 2 * l + i
            outside = jnp.logical_or(jnp.logical_and(sec == 0, f < 2), jnp.logical_or(jnp.logical_and(p == 0, y == 0), jnp.logical_and(p == SEQ - 1, y == 3)))
            for j in range(2):
                x = hid[pl.ds(pl.multiple_of(lf * RC, RC), RC), pl.ds((i * 2 + j) * CH, CH)].astype(jnp.bfloat16).astype(jnp.float32)
                x = x * lax.rsqrt(jnp.mean(x * x, axis=-1, keepdims=True) + EPS) * vg_ref[...]
                x = jnp.where(outside, 0.0, x / (1.0 + jnp.exp(-x)))
                tap[f, y, :, pl.ds((1 + j) * CH, CH)] = x.astype(jnp.bfloat16)
                if j == 0:
                    x = jnp.where(is_last, 0.0, pltpu.roll(x, RC - 1, 0))
                    tap[f, y, :, pl.ds(3 * CH, CH)] = x.astype(jnp.bfloat16)
                else:
                    x = jnp.where(is_first, 0.0, pltpu.roll(x, 1, 0))
                    tap[f, y, :, pl.ds(0, CH)] = x.astype(jnp.bfloat16)
            return 0

        lax.fori_loop(0, 8, activate, 0)

    w_copy.wait()
    cacc[...] = jnp.zeros_like(cacc)

    def one_tap(t, _):
        a, b = lax.div(t, 3), lax.rem(t, 3)
        block = tap[pl.ds(a, 2), pl.ds(b, 2)].reshape(4 * RC, 4 * CH)
        both = jnp.concatenate([block[:, : 3 * CH], block[:, CH:]], axis=0)
        cacc[...] += jnp.dot(both, wconv[t], preferred_element_type=jnp.float32)
        return 0

    lax.fori_loop(0, 9, one_tap, 0)
    for f in range(2):
        for y in range(2):
            rows = pl.ds((y * 4 + 2 + f) * RC, RC)
            for j in range(2):
                hidden = hid[rows, pl.ds(((1 - y) * 2 + j) * CH, CH)].astype(jnp.bfloat16).astype(jnp.float32)
                out = hidden + cacc[pl.ds(((j * 2 + f) * 2 + y) * RC, RC), :]
                dec_ref[f, y, :, pl.ds(j * CH, CH)] = out.astype(jnp.bfloat16)

    arrived(qsrc, ssq)
    arrived(kvsrc, sskv)
    arrived(obuf, sso)
    arrived(xrecv.at[pl.ds(0, 3 * SEC - 1)], ssx)

    def sent(g, _):
        arrived(chunk_of(kvbuf, g), ssf.at[g])
        return 0

    lax.fori_loop(0, CHUNKS, sent, 0)


def shards(
    queries, keys, values, query_gain, key_gain, noisy, head_weight, conv_in_weight, conv_in_bias, vae_gain, conv_weight
):
    rowsel, lanesel = gather_constants()
    vmem = pl.BlockSpec(memory_space=pltpu.VMEM)
    anywhere = pl.BlockSpec(memory_space=pl.ANY)
    bf16, f32, dma = jnp.bfloat16, jnp.float32, pltpu.SemaphoreType.DMA
    latents, decoded = pl.pallas_call(
        kernel,
        out_shape=(jax.ShapeDtypeStruct((ROWS, 64), f32), jax.ShapeDtypeStruct((2, 2, RC, 2 * CH), bf16)),
        in_specs=[vmem] * 6 + [anywhere] + [vmem] * 3 + [anywhere] + [vmem] * 2,
        out_specs=(vmem, vmem),
        scratch_shapes=[
            pltpu.VMEM((HEADS, ROWS, HEAD_DIM), bf16),
            pltpu.VMEM((HEADS, 2, ROWS, HEAD_DIM), bf16),
            pltpu.VMEM((STEPS, ROWS, HEAD_DIM), bf16),
            pltpu.VMEM((STEPS, 2, ROWS, HEAD_DIM), bf16),
            pltpu.VMEM((STEPS, 2, ROWS, HEAD_DIM), bf16),
            pltpu.VMEM((N_QB, HEAD_DIM, QB), f32),
            pltpu.VMEM((N_QB, 8, QB), f32),
            pltpu.VMEM((N_QB, 8, QB), f32),
            pltpu.VMEM((2 * KC, QB), f32),
            pltpu.VMEM((2 * KC, QB), f32),
            pltpu.VMEM((STEPS, HALF, 128), bf16),
            pltpu.VMEM((STEPS, HALF, 128), bf16),
            pltpu.VMEM((HALF, 128), bf16),
            pltpu.VMEM((3 * SEC, HALF, 128), bf16),
            pltpu.VMEM((12, 3, RC, 128), bf16),
            pltpu.VMEM((8 * RC, 768), bf16),
            pltpu.VMEM((8 * RC, 4 * CH), f32),
            pltpu.VMEM((4, 4, RC, 4 * CH), bf16),
            pltpu.VMEM((768, 4 * CH), bf16),
            pltpu.VMEM((9, 3 * CH, CH), bf16),
            pltpu.VMEM((HEAD_DIM, 64), bf16),
            pltpu.VMEM((8 * RC, CH), f32),
            dma, dma, dma((CHUNKS,)), dma, dma, dma, dma((CHUNKS,)), dma((CHUNKS,)), dma, dma, dma((2,)),
        ],
        compiler_params=pltpu.CompilerParams(collective_id=0, has_side_effects=True, vmem_limit_bytes=56 * 2**20),
        name="step",
    )(
        queries[0],
        keys[0],
        values[0],
        query_gain.reshape(1, -1),
        key_gain.reshape(1, -1),
        noisy[0],
        head_weight,
        conv_in_weight.reshape(432, CH),
        conv_in_bias.reshape(1, CH),
        vae_gain.reshape(1, CH),
        conv_weight.reshape(9, 3 * CH, CH),
        jnp.asarray(rowsel, bf16),
        jnp.asarray(lanesel, bf16),
    )
    decoded = decoded.reshape(2, 2, SEC, PCOLS, 2, CH).transpose(2, 0, 1, 3, 4, 5)
    return latents[None], decoded.reshape(SEC, 2, 2, 2 * PCOLS, CH)


def solution(mesh):
    placed = (
        P("sec", "seq", None),
        P("sec", "seq", None),
        P("sec", "seq", None),
        P(),
        P(),
        P("sec", "seq", None),
        P(),
        P(),
        P(),
        P(),
        P(),
    )
    return jax.shard_map(
        shards,
        mesh=mesh,
        in_specs=placed,
        out_specs=(P("sec", "seq", None), P(None, "sec", "seq", None, None)),
        check_vma=False,
    )
```

time: 285 us -> 127 us (0.45)
  the two profiles are of different devices: /device:TPU:9 before, /device:TPU:1 now
where the time goes in v1:
time: 127 us; the launch traced here: 126 us
  Pallas kernels  116 us (91%)
  local copies, waits for them, and re-layouts  9.74 us (8%)
    pallas_call x1, Pallas kernels, shards(): pl.pallas_call(kernel, out_shape=(jax.ShapeDtypeStruct((ROWS, 64), f32),...  116 us
    unnamed x3, local copies, waits for them, and re-layouts  5.34 us

profile of v1, /device:TPU:1, one launch (start us, length us, event | category | flops | bytes accessed | tf_op | source)
XLA Modules:
  0.0 126.5 jit_solution(4635815677293924733)
XLA Ops:
  0.6 1.2 reshape.31.bias_ref
  1.9 1.3 %reshape.32.vg_ref = f32[1,384]{1,0:T(1,128)} reshape(f32[384]{0:T(512)} %param.22) | data formatting | bytes 3072 | tf_op jit(solution)/shard_map/reshape | solution.py:404
  3.1 1.5 %copy.15 = f32[1,96,64]{2,1,0:T(8,128)} copy(f32[1,96,64]{1,2,0:T(8,128)} %param.18) | data formatting | bytes 49152 | tf_op args[5]
  4.6 2.4 %copy.16.hw_ref = bf16[4096,64]{1,0:T(8,128)(2,1)} copy(bf16[4096,64]{0,1:T(8,128)(2,1)} %param.19) | data formatting | bytes 1048576 | tf_op args[6]
  7.0 116.1 %step.1 = (f32[96,64]{1,0:T(8,128)}, bf16[2,2,48,768]{3,2,1,0:T(8,128)(2,1)}) custom-call(bf16[96,4096]{1,0:T(8,128)(2,1)} %bitcast.16, bf16[96,4096]{1,0:T(8,128)(2,1)} %bitcast.17, bf16[96,4096]{1,0:T(8,128)(2,1)} %bitcast.18, f32[1,4096]{1,0:T(1,128)} %bitcast.22, f32[1,4096]{1,0:T(1,128)} %bitcast.23, f32[96,64]{1,0:T(8,128)} %bitcast.20, ...), custom_call_target="tpu_custom_call" | custom-call | tf_op jit(solution)/shard_map/step/pallas_call | solution.py:362
  123.1 1.5 %copy.18 = f32[1,96,64]{1,2,0:T(8,128)} copy(f32[1,96,64]{2,1,0:T(8,128)} %bitcast.21) | data formatting | bytes 49152
  124.6 1.0 reshape.34
  125.6 0.1 reshape.36
  125.7 0.7 copy.19

commit v2 on v1

v2 whole, which is shorter than its diff:
```python
import functools
import math

import jax
import jax.numpy as jnp
import numpy as np
from jax import lax
from jax.experimental import pallas as pl
from jax.experimental.pallas import tpu as pltpu
from jax.sharding import PartitionSpec as P

HEADS = 32
HEAD_DIM = 128
ROWS = 96
HALF = ROWS // 2
SEQ = 64
SEC = 4
STEPS = 32
PER_CHUNK = 4
CHUNKS = STEPS // PER_CHUNK
AHEAD = 2
PER_QB = 8
QB = PER_QB * ROWS
N_QB = STEPS // PER_QB
KC = 2 * PER_CHUNK * ROWS
KV_ROWS = ROWS + HALF
PCOLS = 12
RC = SEC * PCOLS
CH = 384
EPS = 1e-06
MESH = pl.DeviceIdType.MESH
NT = (((1,), (1,)), ((), ()))
LOG2E = 1.0 / math.log(2.0)


def offsets(i):
    b, c = i // 4, i % 4
    return (b // 4 + c // 2) % 2, (b + c) % 4, c


def gather_constants():
    rows = np.zeros((3, 4 * RC, 4 * RC), np.float32)
    lanes = np.zeros((3, 128, 256), np.float32)
    for k in range(3):
        for f in range(4):
            for r in range(SEC):
                for c in range(PCOLS):
                    if 0 <= c + k - 1 < PCOLS:
                        rows[k, (f * SEC + r) * PCOLS + c, (r * 4 + f) * PCOLS + c + k - 1] = 1
    for half in range(2):
        for i in range(2):
            for tap, (k, j) in enumerate(((0, 1), (1, 0), (1, 1), (2, 0))):
                for ch in range(16):
                    lanes[k, half * 64 + i * 32 + j * 16 + ch, half * 128 + i * 64 + tap * 16 + ch] = 1
    return rows, lanes.reshape(384, 256)


def kernel(
    q_hbm, k_hbm, v_hbm, qg_ref, kg_ref, noisy_ref, hw_ref, win_ref, bias_ref, vg_ref, w_ref, rowsel_ref, lanesel_ref,
    lat_ref, dec_ref,
    q_ref, k_ref, v_ref, qsrc, kvsrc, qbuf, kvbuf, sibbuf, keys, values, acc, m_s, l_s, s_a, s_b, obuf, vbuf,
    noisy_s, xsrc, xrecv, xf, lhs, hid, tap, wbig, wconv, cacc, dec_s,
    ssq, sskv, ssf, sso, ssx, rq, rkv, rf, ro, rx, lsem,
):
    sec, p = lax.axis_index("sec"), lax.axis_index("seq")
    z_lo, core = lax.div(sec, 2), lax.rem(sec, 2)
    part, place = lax.div(p, 32), lax.rem(p, 32)
    local = [
        pltpu.make_async_copy(src, dst, lsem.at[n])
        for n, (src, dst) in enumerate(((q_hbm, q_ref), (k_hbm, k_ref), (v_hbm, v_ref), (w_ref, wconv)))
    ]
    for copy in local:
        copy.start()

    place_y, place_x, place_z = lax.div(place, 16), lax.rem(lax.div(place, 4), 4), lax.rem(place, 4)
    ys = [lax.rem(place_y + n, 2) * 16 for n in range(2)]
    xs = [lax.rem(place_x + n, 4) * 4 for n in range(4)]
    zs = [lax.rem(place_z + n, 4) for n in range(4)]

    def target(h):
        return (2 * z_lo + 1 - part, h + 32 * core)

    def source(j):
        return (2 * z_lo + part, j + 32 * (1 - core))

    def head_at(i):
        dy, dx, dz = offsets(i)
        return ys[dy] + xs[dx] + zs[dz]

    def source_at(i):
        dy, dx, dz = offsets(i)
        return source(ys[dy] + xs[-dx % 4] + zs[-dz % 4])

    sibling = (2 * z_lo + 1 - core, p)

    def beside(d):
        return lax.rem(p + SEQ + d, SEQ)

    barrier = pltpu.get_barrier_semaphore()
    for i in range(STEPS):
        pl.semaphore_signal(barrier, inc=1, device_id=target(head_at(i)), device_id_type=MESH)
        pl.semaphore_signal(barrier, inc=1, device_id=source_at(i), device_id_type=MESH)
    pl.semaphore_signal(barrier, inc=1, device_id=sibling, device_id_type=MESH)
    for d in (-1, 0, 1):
        for s in range(1, SEC) if d == 0 else range(SEC):
            pl.semaphore_signal(barrier, inc=1, device_id=(lax.rem(sec + s, SEC), beside(d)), device_id_type=MESH)

    def normed(ref, gain_ref, factor, store):
        def some(t, _):
            rows = pl.ds(pl.multiple_of(t * 16, 16), 16)
            x = ref[rows, :].astype(jnp.float32)
            scale = lax.rsqrt(jnp.mean(x * x, axis=-1, keepdims=True) + EPS)
            for h in range(HEADS):
                cols = slice(h * HEAD_DIM, (h + 1) * HEAD_DIM)
                y = x[:, cols] * scale * gain_ref[:, cols]
                store(h, rows, (y if factor is None else y * factor).astype(jnp.bfloat16))
            return 0

        lax.fori_loop(0, ROWS // 16, some, 0)

    def store_q(h, rows, y):
        qsrc[h, rows, :] = y

    def store_k(h, rows, y):
        kvsrc[h, rows, :] = y

    local[0].wait()
    normed(q_ref, qg_ref, LOG2E / math.sqrt(HEAD_DIM), store_q)
    pl.semaphore_wait(barrier, 2 * STEPS + 1 + 3 * SEC - 1)
    for i in range(STEPS):
        h = head_at(i)
        pltpu.make_async_remote_copy(
            src_ref=qsrc.at[h], dst_ref=qbuf.at[i], send_sem=ssq, recv_sem=rq, device_id=target(h), device_id_type=MESH
        ).start()
    local[1].wait()
    normed(k_ref, kg_ref, None, store_k)
    local[2].wait()
    for h in range(HEADS):
        cols = slice(h * HEAD_DIM, (h + 1) * HEAD_DIM)
        weighted = lax.dot_general(v_ref[:, cols], hw_ref[:, cols], NT, preferred_element_type=jnp.float32)
        kvsrc[h, pl.ds(ROWS, HALF)] = jnp.concatenate([weighted[:HALF], weighted[HALF:]], axis=1).astype(jnp.bfloat16)

    def send_chunk(g):
        for n in range(PER_CHUNK):
            y = lax.rem(place_y + lax.div(g, 4) + n // 2, 2)
            x = lax.rem(place_x + g + n, 4)
            h = y * 16 + x * 4 + zs[n]
            pltpu.make_async_remote_copy(
                src_ref=kvsrc.at[h],
                dst_ref=kvbuf.at[g * PER_CHUNK + n],
                send_sem=sskv,
                recv_sem=rkv.at[g],
                device_id=target(h),
                device_id_type=MESH,
            ).start()

    def arrived(buffer, sem):
        pltpu.make_async_copy(buffer, buffer, sem).wait()

    send_chunk(0)
    wbig[...] = jnp.zeros_like(wbig)
    for a in range(3):
        for b in range(3):
            block = win_ref[pl.ds((a * 3 + b) * 48, 48), :]
            for i in range(2):
                for j in range(2):
                    wbig[pl.ds(a * 256 + (b + i) * 64 + j * 16, 48), pl.ds((i * 2 + j) * CH, CH)] = block
    xf[pl.ds(0, 4)] = jnp.zeros((4,) + xf.shape[1:], jnp.bfloat16)
    noisy = noisy_ref[...].T
    noisy_s[...] = jnp.concatenate([noisy[:HALF], noisy[HALF:]], axis=1)
    acc[...] = jnp.zeros_like(acc)
    l_s[...] = jnp.zeros_like(l_s)
    m_s[...] = jnp.full_like(m_s, -1e30)
    arrived(qsrc, ssq)
    for g in range(1, AHEAD):
        send_chunk(g)

    def chunk_of(buffer, g):
        return buffer.at[pl.ds(g * PER_CHUNK, PER_CHUNK)]

    def pass_on(g):
        arrived(chunk_of(kvbuf, g), rkv.at[g])
        pltpu.make_async_remote_copy(
            src_ref=chunk_of(kvbuf, g),
            dst_ref=chunk_of(sibbuf, g),
            send_sem=ssf.at[g],
            recv_sem=rf.at[g],
            device_id=sibling,
            device_id_type=MESH,
        ).start()

    def take(g):
        arrived(chunk_of(sibbuf, g), rf.at[g])
        steps = pl.ds(g * PER_CHUNK, PER_CHUNK)
        for half in range(2):
            for n, buffer in enumerate((kvbuf, sibbuf)):
                keys[pl.ds((half * 2 + n) * KC // 4, KC // 4), :] = buffer[steps, pl.ds(half * HALF, HALF)].reshape(KC // 4, HEAD_DIM)
        both = jnp.concatenate([buffer[steps, pl.ds(ROWS, HALF)].reshape(KC // 4, 128) for buffer in (kvbuf, sibbuf)], axis=0).T
        values[:, pl.ds(0, KC // 2)] = both[:64]
        values[:, pl.ds(KC // 2, KC // 2)] = both[64:]

    def score(j, dst):
        q = qbuf[pl.ds(j * PER_QB, PER_QB)].reshape(QB, HEAD_DIM)
        dst[...] = lax.dot_general(keys[...], q, NT, preferred_element_type=jnp.float32)

    def update(j, src):
        s = src[...]
        m_old = m_s[j]
        m_new = jnp.maximum(m_old, jnp.max(s, axis=0, keepdims=True))
        m_s[j] = m_new
        alpha = jnp.exp2(m_old - m_new)
        e = jnp.exp2(s - m_new[:1])
        l_s[j] = l_s[j] * alpha + jnp.sum(e.reshape(KC // 8, 8, QB), axis=0)
        acc[j] = acc[j] * alpha[:1] + jnp.dot(values[...], e.astype(jnp.bfloat16), preferred_element_type=jnp.float32)

    def give_back(j):
        total = jnp.sum(l_s[j], axis=0, keepdims=True)
        velocity = (acc[j] * (1.0 / total)).T
        for n in range(PER_QB):
            rows = velocity[n * ROWS : (n + 1) * ROWS]
            i = j * PER_QB + n
            obuf[i] = jnp.concatenate([rows[:HALF], rows[HALF:]], axis=1).astype(jnp.bfloat16)
            pltpu.make_async_remote_copy(
                src_ref=obuf.at[i],
                dst_ref=vbuf.at[i],
                send_sem=sso,
                recv_sem=ro,
                device_id=source_at(i),
                device_id_type=MESH,
            ).start()

    arrived(qbuf, rq)
    pass_on(0)

    def chunk(g, _):
        take(g)

        @pl.when(g + AHEAD < CHUNKS)
        def _():
            send_chunk(g + AHEAD)

        last = g == CHUNKS - 1
        score(0, s_a)
        for i in range(N_QB // 2):
            if i == N_QB // 2 - 1:
                pl.when(jnp.logical_not(last))(lambda: pass_on(g + 1))
            score(2 * i + 1, s_b)
            update(2 * i, s_a)
            pl.when(last)(lambda: give_back(2 * i))
            if i < N_QB // 2 - 1:
                score(2 * i + 2, s_a)
            update(2 * i + 1, s_b)
            pl.when(last)(lambda: give_back(2 * i + 1))
        return 0

    lax.fori_loop(0, CHUNKS, chunk, 0)

    arrived(vbuf, ro)
    latents = noisy_s[...] + jnp.sum(vbuf[...].astype(jnp.float32), axis=0)
    patches = latents.astype(jnp.bfloat16)
    xsrc[...] = patches
    xrecv[SEC + sec] = patches
    for d in (-1, 0, 1):
        for s in range(1, SEC) if d == 0 else range(SEC):
            pltpu.make_async_remote_copy(
                src_ref=xsrc,
                dst_ref=xrecv.at[(1 - d) * SEC + sec],
                send_sem=ssx,
                recv_sem=rx,
                device_id=(lax.rem(sec + s, SEC), beside(d)),
                device_id_type=MESH,
            ).start()
    lat_ref[...] = jnp.concatenate([latents[:, :64], latents[:, 64:]], axis=0).T
    arrived(xrecv.at[pl.ds(0, 3 * SEC - 1)], rx)

    for d in range(3):
        got = xrecv[pl.ds(d * SEC, SEC)].reshape(SEC * HALF, 128)
        shifted = [jnp.dot(rowsel_ref[k], got, preferred_element_type=jnp.float32).astype(jnp.bfloat16) for k in range(3)]
        rows = jnp.dot(jnp.concatenate(shifted, axis=1), lanesel_ref[...], preferred_element_type=jnp.float32)
        if d == 0:
            rows = jnp.where(p == 0, 0.0, rows)
        if d == 2:
            rows = jnp.where(p == SEQ - 1, 0.0, rows)
        rows = rows.astype(jnp.bfloat16)
        for f in range(8):
            xf[4 + f, d] = rows[f % 4 * RC : (f % 4 + 1) * RC, f // 4 * 128 : (f // 4 + 1) * 128]
    for l in range(2):
        for f in range(4):
            for a in range(3):
                for n in range(2):
                    lhs[pl.ds((l * 4 + f) * RC, RC), pl.ds(a * 256 + n * 128, 128)] = xf[2 * sec + f + a, l + n]
    row = lax.broadcasted_iota(jnp.int32, (RC, CH), 0)
    is_first = functools.reduce(jnp.logical_or, [row == r * PCOLS for r in range(SEC)])
    is_last = functools.reduce(jnp.logical_or, [row == r * PCOLS + PCOLS - 1 for r in range(SEC)])
    bias, gain = bias_ref[...].reshape(1, CH), vg_ref[...].reshape(1, CH)

    def convolve(n):
        cols = pl.ds(n * CH, CH)
        hid[:, cols] = jnp.dot(lhs[...], wbig[:, cols], preferred_element_type=jnp.float32) + bias

    def activate(n):
        i, j = n // 2, n % 2
        for l in range(2):
            for f in range(4):
                y = 2 * l + i
                x = hid[pl.ds((l * 4 + f) * RC, RC), pl.ds(n * CH, CH)].astype(jnp.bfloat16).astype(jnp.float32)
                x = x * lax.rsqrt(jnp.mean(x * x, axis=-1, keepdims=True) + EPS) * gain
                x = 0.5 * x
                x = x + x * jnp.tanh(x)
                outside = [sec == 0] * (f < 2) + [p == 0] * (y == 0) + [p == SEQ - 1] * (y == 3)
                if outside:
                    x = jnp.where(functools.reduce(jnp.logical_or, outside), 0.0, x)
                tap[f, y, :, pl.ds((1 + j) * CH, CH)] = x.astype(jnp.bfloat16)
                if j == 0:
                    x = jnp.where(is_last, 0.0, pltpu.roll(x, RC - 1, 0))
                    tap[f, y, :, pl.ds(3 * CH, CH)] = x.astype(jnp.bfloat16)
                else:
                    x = jnp.where(is_first, 0.0, pltpu.roll(x, 1, 0))
                    tap[f, y, :, pl.ds(0, CH)] = x.astype(jnp.bfloat16)

    convolve(0)
    for n in range(4):
        if n < 3:
            convolve(n + 1)
        activate(n)

    local[3].wait()
    cacc[...] = jnp.zeros_like(cacc)

    def one_tap(t, _):
        a, b = lax.div(t, 3), lax.rem(t, 3)
        block = tap[pl.ds(a, 2), pl.ds(b, 2)].reshape(4 * RC, 4 * CH)
        both = jnp.concatenate([block[:, : 3 * CH], block[:, CH:]], axis=0)
        cacc[...] += jnp.dot(both, wconv[t], preferred_element_type=jnp.float32)
        return 0

    lax.fori_loop(0, 9, one_tap, 0)
    for f in range(2):
        for y in range(2):
            rows = pl.ds((y * 4 + 2 + f) * RC, RC)
            for j in range(2):
                hidden = hid[rows, pl.ds(((1 - y) * 2 + j) * CH, CH)].astype(jnp.bfloat16).astype(jnp.float32)
                out = hidden + cacc[pl.ds(((j * 2 + f) * 2 + y) * RC, RC), :]
                for r in range(SEC):
                    for n in range(CH // 128):
                        part_out = out[r * PCOLS : (r + 1) * PCOLS, n * 128 : (n + 1) * 128]
                        dec_s[r, f, y, n, pl.ds(j, PCOLS, 2), :] = part_out
            for r in range(SEC):
                for n in range(CH // 128):
                    dec_ref[r, f, y, :, pl.ds(n * 128, 128)] = dec_s[r, f, y, n].astype(jnp.bfloat16)

    arrived(kvsrc, sskv)
    arrived(obuf, sso)
    arrived(xrecv.at[pl.ds(0, 3 * SEC - 1)], ssx)

    def sent(g, _):
        arrived(chunk_of(kvbuf, g), ssf.at[g])
        return 0

    lax.fori_loop(0, CHUNKS, sent, 0)


def shards(
    queries, keys, values, query_gain, key_gain, noisy, head_weight, conv_in_weight, conv_in_bias, vae_gain, conv_weight
):
    rowsel, lanesel = gather_constants()
    vmem = pl.BlockSpec(memory_space=pltpu.VMEM)
    anywhere = pl.BlockSpec(memory_space=pl.ANY)
    bf16, f32, dma = jnp.bfloat16, jnp.float32, pltpu.SemaphoreType.DMA
    latents, decoded = pl.pallas_call(
        kernel,
        out_shape=(jax.ShapeDtypeStruct((64, ROWS), f32), jax.ShapeDtypeStruct((SEC, 2, 2, 2 * PCOLS, CH), bf16)),
        in_specs=[anywhere] * 3 + [vmem] * 7 + [anywhere] + [vmem] * 2,
        out_specs=(vmem, vmem),
        scratch_shapes=[
            *[pltpu.VMEM((ROWS, HEADS * HEAD_DIM), bf16)] * 3,
            pltpu.VMEM((HEADS, ROWS, HEAD_DIM), bf16),
            pltpu.VMEM((HEADS, KV_ROWS, HEAD_DIM), bf16),
            pltpu.VMEM((STEPS, ROWS, HEAD_DIM), bf16),
            pltpu.VMEM((STEPS, KV_ROWS, HEAD_DIM), bf16),
            pltpu.VMEM((STEPS, KV_ROWS, HEAD_DIM), bf16),
            pltpu.VMEM((KC, HEAD_DIM), bf16),
            pltpu.VMEM((64, KC), bf16),
            pltpu.VMEM((N_QB, 64, QB), f32),
            pltpu.VMEM((N_QB, 8, QB), f32),
            pltpu.VMEM((N_QB, 8, QB), f32),
            pltpu.VMEM((KC, QB), f32),
            pltpu.VMEM((KC, QB), f32),
            pltpu.VMEM((STEPS, HALF, 128), bf16),
            pltpu.VMEM((STEPS, HALF, 128), bf16),
            pltpu.VMEM((HALF, 128), f32),
            pltpu.VMEM((HALF, 128), bf16),
            pltpu.VMEM((3 * SEC, HALF, 128), bf16),
            pltpu.VMEM((12, 3, RC, 128), bf16),
            pltpu.VMEM((8 * RC, 768), bf16),
            pltpu.VMEM((8 * RC, 4 * CH), f32),
            pltpu.VMEM((4, 4, RC, 4 * CH), bf16),
            pltpu.VMEM((768, 4 * CH), bf16),
            pltpu.VMEM((9, 3 * CH, CH), bf16),
            pltpu.VMEM((8 * RC, CH), f32),
            pltpu.VMEM((SEC, 2, 2, CH // 128, 2 * PCOLS, 128), f32),
            dma, dma, dma((CHUNKS,)), dma, dma, dma, dma((CHUNKS,)), dma((CHUNKS,)), dma, dma, dma((4,)),
        ],
        compiler_params=pltpu.CompilerParams(collective_id=0, has_side_effects=True, vmem_limit_bytes=56 * 2**20),
        name="step",
    )(
        queries[0],
        keys[0],
        values[0],
        query_gain.reshape(1, -1),
        key_gain.reshape(1, -1),
        noisy[0].T,
        head_weight.T,
        conv_in_weight.reshape(432, CH),
        conv_in_bias,
        vae_gain,
        conv_weight.reshape(9, 3 * CH, CH),
        jnp.asarray(rowsel, bf16),
        jnp.asarray(lanesel, bf16),
    )
    return latents.T[None], decoded


def solution(mesh):
    placed = (
        P("sec", "seq", None),
        P("sec", "seq", None),
        P("sec", "seq", None),
        P(),
        P(),
        P("sec", "seq", None),
        P(),
        P(),
        P(),
        P(),
        P(),
    )
    return jax.shard_map(
        shards,
        mesh=mesh,
        in_specs=placed,
        out_specs=(P("sec", "seq", None), P(None, "sec", "seq", None, None)),
        check_vma=False,
    )
```

time: 127 us -> 108 us (0.85)
  Pallas kernels: 116 us -> 104 us
  local copies, waits for them, and re-layouts: 9.74 us -> 3.08 us
    pallas_call x1, Pallas kernels: 116 us -> 104 us  [shards(): pl.pallas_call(kernel, out_shape=(jax.ShapeDtypeStruct((64, ROWS), f32),...]
    reshape x5 -> x0, local copies, waits for them, and re-layouts: 4.41 us -> none  [the longest x1 1.27 us: shards(): vae_gain.reshape(1, CH)]
    unnamed x3 -> x2, local copies, waits for them, and re-layouts: 5.34 us -> 3.08 us
where the time goes in v2:
time: 108 us; the launch traced here: 107 us
  Pallas kernels  104 us (96%)
  local copies, waits for them, and re-layouts  3.08 us (3%)
    pallas_call x1, Pallas kernels, shards(): pl.pallas_call(kernel, out_shape=(jax.ShapeDtypeStruct((64, ROWS), f32),...  104 us
    unnamed x2, local copies, waits for them, and re-layouts  3.08 us

profile of v2, /device:TPU:1, one launch (start us, length us, event | category | flops | bytes accessed | tf_op | source)
XLA Modules:
  0.0 107.4 jit_solution(17826172159231825553)
XLA Ops:
  0.6 103.6 %step.1 = (f32[64,96]{1,0:T(8,128)}, bf16[4,2,2,24,384]{4,3,2,1,0:T(8,128)(2,1)}) custom-call(bf16[96,4096]{1,0:T(8,128)(2,1)} %bitcast.15, bf16[96,4096]{1,0:T(8,128)(2,1)} %bitcast.16, bf16[96,4096]{1,0:T(8,128)(2,1)} %bitcast.17, f32[1,4096]{1,0:T(1,128)} %bitcast.22, f32[1,4096]{1,0:T(1,128)} %bitcast.23, f32[64,96]{1,0:T(8,128)} %bitcast.20, ...), custom_call_target="tpu_custom_call" | custom-call | tf_op jit(solution)/shard_map/step/pallas_call | solution.py:370
  104.3 1.4 %copy.17 = f32[1,96,64]{1,2,0:T(8,128)} copy(f32[1,96,64]{1,2,0:T(8,128)} %bitcast.21) | data formatting | bytes 49152
  105.7 1.7 %copy.18 = bf16[4,2,2,24,384]{4,3,2,1,0:T(8,128)(2,1)} copy(bf16[4,2,2,24,384]{4,3,2,1,0:T(8,128)(2,1)} %get-tuple-element.9) | data formatting | bytes 589824

commit v3 on v2

--- a/solution.py
+++ b/solution.py
@@ -18,10 +18,11 @@
 STEPS = 32
 PER_CHUNK = 4
 CHUNKS = STEPS // PER_CHUNK
-AHEAD = 2
+AHEAD = 3
 PER_QB = 8
 QB = PER_QB * ROWS
 N_QB = STEPS // PER_QB
+PEERS = STEPS // 4
 KC = 2 * PER_CHUNK * ROWS
 KV_ROWS = ROWS + HALF
 PCOLS = 12
@@ -58,9 +59,9 @@
 def kernel(
     q_hbm, k_hbm, v_hbm, qg_ref, kg_ref, noisy_ref, hw_ref, win_ref, bias_ref, vg_ref, w_ref, rowsel_ref, lanesel_ref,
     lat_ref, dec_ref,
-    q_ref, k_ref, v_ref, qsrc, kvsrc, qbuf, kvbuf, sibbuf, keys, values, acc, m_s, l_s, s_a, s_b, obuf, vbuf,
+    q_ref, k_ref, v_ref, qsrc, kvsrc, qbuf, kvbuf, sibbuf, keys, values, acc, m_s, l_s, s_a, s_b, gsrc, gbuf, hsrc, vbuf,
     noisy_s, xsrc, xrecv, xf, lhs, hid, tap, wbig, wconv, cacc, dec_s,
-    ssq, sskv, ssf, sso, ssx, rq, rkv, rf, ro, rx, lsem,
+    ssq, sskv, ssf, sso, ssh, ssx, rq, rkv, rf, ro, rh, rx, lsem,
 ):
     sec, p = lax.axis_index("sec"), lax.axis_index("seq")
     z_lo, core = lax.div(sec, 2), lax.rem(sec, 2)
@@ -69,7 +70,7 @@
         pltpu.make_async_copy(src, dst, lsem.at[n])
         for n, (src, dst) in enumerate(((q_hbm, q_ref), (k_hbm, k_ref), (v_hbm, v_ref), (w_ref, wconv)))
     ]
-    for copy in local:
+    for copy in local[:3]:
         copy.start()
 
     place_y, place_x, place_z = lax.div(place, 16), lax.rem(lax.div(place, 4), 4), lax.rem(place, 4)
@@ -90,6 +91,9 @@
     def source_at(i):
         dy, dx, dz = offsets(i)
         return source(ys[dy] + xs[-dx % 4] + zs[-dz % 4])
+
+    def peer_at(e):
+        return (sec, ys[e // 4] + xs[-e % 4] + place_z + 32 * part)
 
     sibling = (2 * z_lo + 1 - core, p)
 
@@ -101,6 +105,8 @@
         pl.semaphore_signal(barrier, inc=1, device_id=target(head_at(i)), device_id_type=MESH)
         pl.semaphore_signal(barrier, inc=1, device_id=source_at(i), device_id_type=MESH)
     pl.semaphore_signal(barrier, inc=1, device_id=sibling, device_id_type=MESH)
+    for e in range(1, PEERS):
+        pl.semaphore_signal(barrier, inc=1, device_id=peer_at(e), device_id_type=MESH)
     for d in (-1, 0, 1):
         for s in range(1, SEC) if d == 0 else range(SEC):
             pl.semaphore_signal(barrier, inc=1, device_id=(lax.rem(sec + s, SEC), beside(d)), device_id_type=MESH)
@@ -126,12 +132,13 @@
 
     local[0].wait()
     normed(q_ref, qg_ref, LOG2E / math.sqrt(HEAD_DIM), store_q)
-    pl.semaphore_wait(barrier, 2 * STEPS + 1 + 3 * SEC - 1)
+    pl.semaphore_wait(barrier, 2 * STEPS + 1 + PEERS - 1 + 3 * SEC - 1)
     for i in range(STEPS):
-        h = head_at(i)
+        h = ys[i // 16] + xs[i // 4 % 4] + zs[i % 4]
         pltpu.make_async_remote_copy(
             src_ref=qsrc.at[h], dst_ref=qbuf.at[i], send_sem=ssq, recv_sem=rq, device_id=target(h), device_id_type=MESH
         ).start()
+    local[3].start()
     local[1].wait()
     normed(k_ref, kg_ref, None, store_k)
     local[2].wait()
@@ -216,18 +223,16 @@
     def give_back(j):
         total = jnp.sum(l_s[j], axis=0, keepdims=True)
         velocity = (acc[j] * (1.0 / total)).T
-        for n in range(PER_QB):
-            rows = velocity[n * ROWS : (n + 1) * ROWS]
-            i = j * PER_QB + n
-            obuf[i] = jnp.concatenate([rows[:HALF], rows[HALF:]], axis=1).astype(jnp.bfloat16)
-            pltpu.make_async_remote_copy(
-                src_ref=obuf.at[i],
-                dst_ref=vbuf.at[i],
-                send_sem=sso,
-                recv_sem=ro,
-                device_id=source_at(i),
-                device_id_type=MESH,
-            ).start()
+        for e in range(j * PER_QB // 4, (j + 1) * PER_QB // 4):
+            to = gbuf if e == 0 else gsrc
+            for dz in range(4):
+                n = e * 4 + dz - j * PER_QB
+                rows = velocity[n * ROWS : (n + 1) * ROWS]
+                to[e, dz] = jnp.concatenate([rows[:HALF], rows[HALF:]], axis=1).astype(jnp.bfloat16)
+            if e:
+                pltpu.make_async_remote_copy(
+                    src_ref=gsrc.at[e], dst_ref=gbuf.at[e], send_sem=sso, recv_sem=ro, device_id=peer_at(e), device_id_type=MESH
+                ).start()
 
     arrived(qbuf, rq)
     pass_on(0)
@@ -255,7 +260,18 @@
 
     lax.fori_loop(0, CHUNKS, chunk, 0)
 
-    arrived(vbuf, ro)
+    arrived(gbuf.at[pl.ds(1, PEERS - 1)], ro)
+    hsrc[...] = jnp.sum(gbuf[...].astype(jnp.float32), axis=0).astype(jnp.bfloat16)
+    for dz in range(4):
+        pltpu.make_async_remote_copy(
+            src_ref=hsrc.at[dz],
+            dst_ref=vbuf.at[dz],
+            send_sem=ssh,
+            recv_sem=rh,
+            device_id=source(ys[0] + xs[0] + zs[-dz % 4]),
+            device_id_type=MESH,
+        ).start()
+    arrived(vbuf, rh)
     latents = noisy_s[...] + jnp.sum(vbuf[...].astype(jnp.float32), axis=0)
     patches = latents.astype(jnp.bfloat16)
     xsrc[...] = patches
@@ -325,16 +341,15 @@
         activate(n)
 
     local[3].wait()
-    cacc[...] = jnp.zeros_like(cacc)
-
-    def one_tap(t, _):
-        a, b = lax.div(t, 3), lax.rem(t, 3)
+    def one_tap(t):
+        a, b = t // 3, t % 3
         block = tap[pl.ds(a, 2), pl.ds(b, 2)].reshape(4 * RC, 4 * CH)
         both = jnp.concatenate([block[:, : 3 * CH], block[:, CH:]], axis=0)
-        cacc[...] += jnp.dot(both, wconv[t], preferred_element_type=jnp.float32)
-        return 0
-
-    lax.fori_loop(0, 9, one_tap, 0)
+        return jnp.dot(both, wconv[t], preferred_element_type=jnp.float32)
+
+    cacc[...] = one_tap(0) + one_tap(1) + one_tap(2)
+    cacc[...] += one_tap(3) + one_tap(4) + one_tap(5)
+    cacc[...] += one_tap(6) + one_tap(7) + one_tap(8)
     for f in range(2):
         for y in range(2):
             rows = pl.ds((y * 4 + 2 + f) * RC, RC)
@@ -350,7 +365,8 @@
                     dec_ref[r, f, y, :, pl.ds(n * 128, 128)] = dec_s[r, f, y, n].astype(jnp.bfloat16)
 
     arrived(kvsrc, sskv)
-    arrived(obuf, sso)
+    arrived(gsrc.at[pl.ds(1, PEERS - 1)], sso)
+    arrived(hsrc, ssh)
     arrived(xrecv.at[pl.ds(0, 3 * SEC - 1)], ssx)
 
     def sent(g, _):
@@ -386,8 +402,8 @@
             pltpu.VMEM((N_QB, 8, QB), f32),
             pltpu.VMEM((KC, QB), f32),
             pltpu.VMEM((KC, QB), f32),
-            pltpu.VMEM((STEPS, HALF, 128), bf16),
-            pltpu.VMEM((STEPS, HALF, 128), bf16),
+            *[pltpu.VMEM((PEERS, 4, HALF, 128), bf16)] * 2,
+            *[pltpu.VMEM((4, HALF, 128), bf16)] * 2,
             pltpu.VMEM((HALF, 128), f32),
             pltpu.VMEM((HALF, 128), bf16),
             pltpu.VMEM((3 * SEC, HALF, 128), bf16),
@@ -399,7 +415,7 @@
             pltpu.VMEM((9, 3 * CH, CH), bf16),
             pltpu.VMEM((8 * RC, CH), f32),
             pltpu.VMEM((SEC, 2, 2, CH // 128, 2 * PCOLS, 128), f32),
-            dma, dma, dma((CHUNKS,)), dma, dma, dma, dma((CHUNKS,)), dma((CHUNKS,)), dma, dma, dma((4,)),
+            dma, dma, dma((CHUNKS,)), dma, dma, dma, dma, dma((CHUNKS,)), dma((CHUNKS,)), dma, dma, dma, dma((4,)),
         ],
         compiler_params=pltpu.CompilerParams(collective_id=0, has_side_effects=True, vmem_limit_bytes=56 * 2**20),
         name="step",

time: 108 us -> 102 us (0.944)
  Pallas kernels: 104 us -> 97.8 us
    pallas_call x1, Pallas kernels: 104 us -> 97.8 us  [shards(): pl.pallas_call(kernel, out_shape=(jax.ShapeDtypeStruct((64, ROWS), f32),...]
where the time goes in v3:
time: 102 us
  Pallas kernels  97.8 us (96%)
  local copies, waits for them, and re-layouts  3.08 us (3%)
    pallas_call x1, Pallas kernels, shards(): pl.pallas_call(kernel, out_shape=(jax.ShapeDtypeStruct((64, ROWS), f32),...  97.8 us
    unnamed x2, local copies, waits for them, and re-layouts  3.08 us

profile of v3, /device:TPU:1, one launch (start us, length us, event | category | flops | bytes accessed | tf_op | source)
XLA Modules:
  0.0 101.5 jit_solution(12410386698005245452)
XLA Ops:
  0.6 97.8 %step.1 = (f32[64,96]{1,0:T(8,128)}, bf16[4,2,2,24,384]{4,3,2,1,0:T(8,128)(2,1)}) custom-call(bf16[96,4096]{1,0:T(8,128)(2,1)} %bitcast.15, bf16[96,4096]{1,0:T(8,128)(2,1)} %bitcast.16, bf16[96,4096]{1,0:T(8,128)(2,1)} %bitcast.17, f32[1,4096]{1,0:T(1,128)} %bitcast.22, f32[1,4096]{1,0:T(1,128)} %bitcast.23, f32[64,96]{1,0:T(8,128)} %bitcast.20, ...), custom_call_target="tpu_custom_call" | custom-call | tf_op jit(solution)/shard_map/step/pallas_call | solution.py:386
  98.5 1.4 %copy.17 = f32[1,96,64]{1,2,0:T(8,128)} copy(f32[1,96,64]{1,2,0:T(8,128)} %bitcast.21) | data formatting | bytes 49152
  99.8 1.7 %copy.18 = bf16[4,2,2,24,384]{4,3,2,1,0:T(8,128)(2,1)} copy(bf16[4,2,2,24,384]{4,3,2,1,0:T(8,128)(2,1)} %get-tuple-element.9) | data formatting | bytes 589824

commit v4 on v3

--- a/solution.py
+++ b/solution.py
@@ -57,20 +57,24 @@
 
 
 def kernel(
-    q_hbm, k_hbm, v_hbm, qg_ref, kg_ref, noisy_ref, hw_ref, win_ref, bias_ref, vg_ref, w_ref, rowsel_ref, lanesel_ref,
+    q_hbm, k_hbm, v_hbm, qg_ref, kg_ref, noisy_ref, hw_hbm, win_hbm, bias_ref, vg_ref, w_hbm, rowsel_hbm, lanesel_hbm,
     lat_ref, dec_ref,
-    q_ref, k_ref, v_ref, qsrc, kvsrc, qbuf, kvbuf, sibbuf, keys, values, acc, m_s, l_s, s_a, s_b, gsrc, gbuf, hsrc, vbuf,
-    noisy_s, xsrc, xrecv, xf, lhs, hid, tap, wbig, wconv, cacc, dec_s,
+    q_ref, k_ref, v_ref, hw_ref, win_ref, wconv, rowsel_ref, lanesel_ref, qsrc, kvsrc, qbuf, kvbuf, sibbuf, keys, values, acc, m_s, l_s, s_a, s_b, gsrc, gbuf, hsrc, vbuf,
+    noisy_s, xsrc, xrecv, xf, lhs, hid, tap, wbig, cacc, dec_s,
     ssq, sskv, ssf, sso, ssh, ssx, rq, rkv, rf, ro, rh, rx, lsem,
 ):
     sec, p = lax.axis_index("sec"), lax.axis_index("seq")
     z_lo, core = lax.div(sec, 2), lax.rem(sec, 2)
     part, place = lax.div(p, 32), lax.rem(p, 32)
+    loads = (
+        (q_hbm, q_ref), (k_hbm, k_ref), (v_hbm, v_ref), (hw_hbm, hw_ref),
+        (win_hbm, win_ref), (rowsel_hbm, rowsel_ref), (lanesel_hbm, lanesel_ref), (w_hbm, wconv),
+    )
     local = [
         pltpu.make_async_copy(src, dst, lsem.at[n])
-        for n, (src, dst) in enumerate(((q_hbm, q_ref), (k_hbm, k_ref), (v_hbm, v_ref), (w_ref, wconv)))
+        for n, (src, dst) in enumerate(loads)
     ]
-    for copy in local[:3]:
+    for copy in local[:4]:
         copy.start()
 
     place_y, place_x, place_z = lax.div(place, 16), lax.rem(lax.div(place, 4), 4), lax.rem(place, 4)
@@ -102,11 +106,7 @@
 
     barrier = pltpu.get_barrier_semaphore()
     for i in range(STEPS):
-        pl.semaphore_signal(barrier, inc=1, device_id=target(head_at(i)), device_id_type=MESH)
         pl.semaphore_signal(barrier, inc=1, device_id=source_at(i), device_id_type=MESH)
-    pl.semaphore_signal(barrier, inc=1, device_id=sibling, device_id_type=MESH)
-    for e in range(1, PEERS):
-        pl.semaphore_signal(barrier, inc=1, device_id=peer_at(e), device_id_type=MESH)
     for d in (-1, 0, 1):
         for s in range(1, SEC) if d == 0 else range(SEC):
             pl.semaphore_signal(barrier, inc=1, device_id=(lax.rem(sec + s, SEC), beside(d)), device_id_type=MESH)
@@ -132,16 +132,18 @@
 
     local[0].wait()
     normed(q_ref, qg_ref, LOG2E / math.sqrt(HEAD_DIM), store_q)
-    pl.semaphore_wait(barrier, 2 * STEPS + 1 + PEERS - 1 + 3 * SEC - 1)
+    pl.semaphore_wait(barrier, STEPS + 3 * SEC - 1)
     for i in range(STEPS):
         h = ys[i // 16] + xs[i // 4 % 4] + zs[i % 4]
         pltpu.make_async_remote_copy(
             src_ref=qsrc.at[h], dst_ref=qbuf.at[i], send_sem=ssq, recv_sem=rq, device_id=target(h), device_id_type=MESH
         ).start()
-    local[3].start()
+    for copy in local[4:]:
+        copy.start()
     local[1].wait()
     normed(k_ref, kg_ref, None, store_k)
     local[2].wait()
+    local[3].wait()
     for h in range(HEADS):
         cols = slice(h * HEAD_DIM, (h + 1) * HEAD_DIM)
         weighted = lax.dot_general(v_ref[:, cols], hw_ref[:, cols], NT, preferred_element_type=jnp.float32)
@@ -166,6 +168,7 @@
 
     send_chunk(0)
     wbig[...] = jnp.zeros_like(wbig)
+    local[4].wait()
     for a in range(3):
         for b in range(3):
             block = win_ref[pl.ds((a * 3 + b) * 48, 48), :]
@@ -289,6 +292,8 @@
     lat_ref[...] = jnp.concatenate([latents[:, :64], latents[:, 64:]], axis=0).T
     arrived(xrecv.at[pl.ds(0, 3 * SEC - 1)], rx)
 
+    local[5].wait()
+    local[6].wait()
     for d in range(3):
         got = xrecv[pl.ds(d * SEC, SEC)].reshape(SEC * HALF, 128)
         shifted = [jnp.dot(rowsel_ref[k], got, preferred_element_type=jnp.float32).astype(jnp.bfloat16) for k in range(3)]
@@ -340,7 +345,7 @@
             convolve(n + 1)
         activate(n)
 
-    local[3].wait()
+    local[7].wait()
     def one_tap(t):
         a, b = t // 3, t % 3
         block = tap[pl.ds(a, 2), pl.ds(b, 2)].reshape(4 * RC, 4 * CH)
@@ -376,6 +381,14 @@
     lax.fori_loop(0, CHUNKS, sent, 0)
 
 
+def hand_on(lat_ref, dec_ref, lat_out, dec_out, sems):
+    copies = [pltpu.make_async_copy(lat_ref, lat_out, sems.at[0]), pltpu.make_async_copy(dec_ref, dec_out, sems.at[1])]
+    for copy in copies:
+        copy.start()
+    for copy in copies:
+        copy.wait()
+
+
 def shards(
     queries, keys, values, query_gain, key_gain, noisy, head_weight, conv_in_weight, conv_in_bias, vae_gain, conv_weight
 ):
@@ -386,10 +399,15 @@
     latents, decoded = pl.pallas_call(
         kernel,
         out_shape=(jax.ShapeDtypeStruct((64, ROWS), f32), jax.ShapeDtypeStruct((SEC, 2, 2, 2 * PCOLS, CH), bf16)),
-        in_specs=[anywhere] * 3 + [vmem] * 7 + [anywhere] + [vmem] * 2,
+        in_specs=[anywhere] * 3 + [vmem] * 3 + [anywhere] * 2 + [vmem] * 2 + [anywhere] * 3,
         out_specs=(vmem, vmem),
         scratch_shapes=[
             *[pltpu.VMEM((ROWS, HEADS * HEAD_DIM), bf16)] * 3,
+            pltpu.VMEM((64, HEADS * HEAD_DIM), bf16),
+            pltpu.VMEM((432, CH), bf16),
+            pltpu.VMEM((9, 3 * CH, CH), bf16),
+            pltpu.VMEM((3, 4 * RC, 4 * RC), bf16),
+            pltpu.VMEM((384, 256), bf16),
             pltpu.VMEM((HEADS, ROWS, HEAD_DIM), bf16),
             pltpu.VMEM((HEADS, KV_ROWS, HEAD_DIM), bf16),
             pltpu.VMEM((STEPS, ROWS, HEAD_DIM), bf16),
@@ -412,10 +430,9 @@
             pltpu.VMEM((8 * RC, 4 * CH), f32),
             pltpu.VMEM((4, 4, RC, 4 * CH), bf16),
             pltpu.VMEM((768, 4 * CH), bf16),
-            pltpu.VMEM((9, 3 * CH, CH), bf16),
             pltpu.VMEM((8 * RC, CH), f32),
             pltpu.VMEM((SEC, 2, 2, CH // 128, 2 * PCOLS, 128), f32),
-            dma, dma, dma((CHUNKS,)), dma, dma, dma, dma, dma((CHUNKS,)), dma((CHUNKS,)), dma, dma, dma, dma((4,)),
+            dma, dma, dma((CHUNKS,)), dma, dma, dma, dma, dma((CHUNKS,)), dma((CHUNKS,)), dma, dma, dma, dma((8,)),
         ],
         compiler_params=pltpu.CompilerParams(collective_id=0, has_side_effects=True, vmem_limit_bytes=56 * 2**20),
         name="step",
@@ -434,6 +451,14 @@
         jnp.asarray(rowsel, bf16),
         jnp.asarray(lanesel, bf16),
     )
+    latents, decoded = pl.pallas_call(
+        hand_on,
+        out_shape=(jax.ShapeDtypeStruct(latents.shape, f32), jax.ShapeDtypeStruct(decoded.shape, bf16)),
+        in_specs=[pl.BlockSpec(memory_space=pltpu.HBM)] * 2,
+        out_specs=(anywhere, anywhere),
+        scratch_shapes=[dma((2,))],
+        name="hand_on",
+    )(latents, decoded)
     return latents.T[None], decoded
 
 

time: 102 us -> 108 us (1.059)
  Pallas kernels: 97.8 us -> 107 us
  local copies, waits for them, and re-layouts: 3.08 us -> 0 us
    pallas_call x0 -> x1, Pallas kernels: none -> 11 us  [shards(): pl.pallas_call(hand_on, out_shape=(jax.ShapeDtypeStruct(latents.shape, f3...]
    unnamed x2 -> x0, local copies, waits for them, and re-layouts: 3.08 us -> none
    pallas_call x1, Pallas kernels: 97.8 us -> 96.1 us  [shards(): pl.pallas_call(kernel, out_shape=(jax.ShapeDtypeStruct((64, ROWS), f32),...]
where the time goes in v4:
time: 108 us
  Pallas kernels  107 us (99%)
    pallas_call x1, Pallas kernels, shards(): pl.pallas_call(kernel, out_shape=(jax.ShapeDtypeStruct((64, ROWS), f32),...  96.1 us
    pallas_call x1, Pallas kernels, shards(): pl.pallas_call(hand_on, out_shape=(jax.ShapeDtypeStruct(latents.shape, f3...  11 us

profile of v4, /device:TPU:1, one launch (start us, length us, event | category | flops | bytes accessed | tf_op | source)
XLA Modules:
  0.0 107.8 jit_solution(5825819817042151240)
XLA Ops:
  0.6 96.1 %step.1 = (f32[64,96]{1,0:T(8,128)}, bf16[4,2,2,24,384]{4,3,2,1,0:T(8,128)(2,1)}) custom-call(bf16[96,4096]{1,0:T(8,128)(2,1)} %bitcast.15, bf16[96,4096]{1,0:T(8,128)(2,1)} %bitcast.16, bf16[96,4096]{1,0:T(8,128)(2,1)} %bitcast.17, f32[1,4096]{1,0:T(1,128)} %bitcast.21, f32[1,4096]{1,0:T(1,128)} %bitcast.22, f32[64,96]{1,0:T(8,128)} %bitcast.20, ...), custom_call_target="tpu_custom_call" | custom-call | tf_op jit(solution)/shard_map/step/pallas_call | solution.py:399
  96.8 11.0 %hand_on.1 = (f32[64,96]{1,0:T(8,128)}, bf16[4,2,2,24,384]{4,3,2,1,0:T(8,128)(2,1)}) custom-call(f32[64,96]{1,0:T(8,128)} %get-tuple-element.6.lat_ref, bf16[4,2,2,24,384]{4,3,2,1,0:T(8,128)(2,1)} %get-tuple-element.7.dec_ref), custom_call_target="tpu_custom_call" | custom-call | tf_op jit(solution)/shard_map/hand_on/pallas_call | solution.py:454

commit v5 on v4

--- a/solution.py
+++ b/solution.py
@@ -18,7 +18,7 @@
 STEPS = 32
 PER_CHUNK = 4
 CHUNKS = STEPS // PER_CHUNK
-AHEAD = 3
+EARLY = CHUNKS // 2
 PER_QB = 8
 QB = PER_QB * ROWS
 N_QB = STEPS // PER_QB
@@ -97,7 +97,9 @@
         return source(ys[dy] + xs[-dx % 4] + zs[-dz % 4])
 
     def peer_at(e):
-        return (sec, ys[e // 4] + xs[-e % 4] + place_z + 32 * part)
+        y = lax.rem(place_y + lax.div(e, 4), 2)
+        x = lax.rem(place_x + 8 - e, 4)
+        return (sec, y * 16 + x * 4 + place_z + 32 * part)
 
     sibling = (2 * z_lo + 1 - core, p)
 
@@ -133,11 +135,20 @@
     local[0].wait()
     normed(q_ref, qg_ref, LOG2E / math.sqrt(HEAD_DIM), store_q)
     pl.semaphore_wait(barrier, STEPS + 3 * SEC - 1)
-    for i in range(STEPS):
-        h = ys[i // 16] + xs[i // 4 % 4] + zs[i % 4]
-        pltpu.make_async_remote_copy(
-            src_ref=qsrc.at[h], dst_ref=qbuf.at[i], send_sem=ssq, recv_sem=rq, device_id=target(h), device_id_type=MESH
-        ).start()
+    def send_queries(j):
+        for n in range(PER_QB):
+            e, i = 2 * j + n // 4, j * PER_QB + n
+            h = lax.rem(place_y + lax.div(e, 4), 2) * 16 + lax.rem(place_x + e, 4) * 4 + zs[n % 4]
+            pltpu.make_async_remote_copy(
+                src_ref=qsrc.at[h],
+                dst_ref=qbuf.at[i],
+                send_sem=ssq.at[j],
+                recv_sem=rq.at[j],
+                device_id=target(h),
+                device_id_type=MESH,
+            ).start()
+
+    send_queries(0)
     for copy in local[4:]:
         copy.start()
     local[1].wait()
@@ -157,7 +168,7 @@
             pltpu.make_async_remote_copy(
                 src_ref=kvsrc.at[h],
                 dst_ref=kvbuf.at[g * PER_CHUNK + n],
-                send_sem=sskv,
+                send_sem=sskv.at[g],
                 recv_sem=rkv.at[g],
                 device_id=target(h),
                 device_id_type=MESH,
@@ -166,7 +177,20 @@
     def arrived(buffer, sem):
         pltpu.make_async_copy(buffer, buffer, sem).wait()
 
+    def chunk_of(buffer, g):
+        return buffer.at[pl.ds(g * PER_CHUNK, PER_CHUNK)]
+
+    def queries_of(buffer, j):
+        return buffer.at[pl.ds(j * PER_QB, PER_QB)]
+
+    def sent_queries(j):
+        arrived(queries_of(qsrc, j), ssq.at[j])
+
+    def sent_chunk(g):
+        arrived(chunk_of(kvsrc, g), sskv.at[g])
+
     send_chunk(0)
+    send_chunk(1)
     wbig[...] = jnp.zeros_like(wbig)
     local[4].wait()
     for a in range(3):
@@ -181,12 +205,12 @@
     acc[...] = jnp.zeros_like(acc)
     l_s[...] = jnp.zeros_like(l_s)
     m_s[...] = jnp.full_like(m_s, -1e30)
-    arrived(qsrc, ssq)
-    for g in range(1, AHEAD):
-        send_chunk(g)
-
-    def chunk_of(buffer, g):
-        return buffer.at[pl.ds(g * PER_CHUNK, PER_CHUNK)]
+    sent_queries(0)
+    send_chunk(2)
+    sent_chunk(0)
+    send_chunk(3)
+    sent_chunk(1)
+    send_queries(1)
 
     def pass_on(g):
         arrived(chunk_of(kvbuf, g), rkv.at[g])
@@ -204,16 +228,16 @@
         steps = pl.ds(g * PER_CHUNK, PER_CHUNK)
         for half in range(2):
             for n, buffer in enumerate((kvbuf, sibbuf)):
-                keys[pl.ds((half * 2 + n) * KC // 4, KC // 4), :] = buffer[steps, pl.ds(half * HALF, HALF)].reshape(KC // 4, HEAD_DIM)
+                keys[g, pl.ds((half * 2 + n) * KC // 4, KC // 4), :] = buffer[steps, pl.ds(half * HALF, HALF)].reshape(KC // 4, HEAD_DIM)
         both = jnp.concatenate([buffer[steps, pl.ds(ROWS, HALF)].reshape(KC // 4, 128) for buffer in (kvbuf, sibbuf)], axis=0).T
-        values[:, pl.ds(0, KC // 2)] = both[:64]
-        values[:, pl.ds(KC // 2, KC // 2)] = both[64:]
-
-    def score(j, dst):
+        values[g, :, pl.ds(0, KC // 2)] = both[:64]
+        values[g, :, pl.ds(KC // 2, KC // 2)] = both[64:]
+
+    def score(g, j, dst):
         q = qbuf[pl.ds(j * PER_QB, PER_QB)].reshape(QB, HEAD_DIM)
-        dst[...] = lax.dot_general(keys[...], q, NT, preferred_element_type=jnp.float32)
-
-    def update(j, src):
+        dst[...] = lax.dot_general(keys[g], q, NT, preferred_element_type=jnp.float32)
+
+    def update(g, j, src):
         s = src[...]
         m_old = m_s[j]
         m_new = jnp.maximum(m_old, jnp.max(s, axis=0, keepdims=True))
@@ -221,47 +245,92 @@
         alpha = jnp.exp2(m_old - m_new)
         e = jnp.exp2(s - m_new[:1])
         l_s[j] = l_s[j] * alpha + jnp.sum(e.reshape(KC // 8, 8, QB), axis=0)
-        acc[j] = acc[j] * alpha[:1] + jnp.dot(values[...], e.astype(jnp.bfloat16), preferred_element_type=jnp.float32)
+        acc[j] = acc[j] * alpha[:1] + jnp.dot(values[g], e.astype(jnp.bfloat16), preferred_element_type=jnp.float32)
 
     def give_back(j):
         total = jnp.sum(l_s[j], axis=0, keepdims=True)
         velocity = (acc[j] * (1.0 / total)).T
-        for e in range(j * PER_QB // 4, (j + 1) * PER_QB // 4):
-            to = gbuf if e == 0 else gsrc
+        for u in range(PER_QB // 4):
+            e = j * (PER_QB // 4) + u
             for dz in range(4):
-                n = e * 4 + dz - j * PER_QB
-                rows = velocity[n * ROWS : (n + 1) * ROWS]
-                to[e, dz] = jnp.concatenate([rows[:HALF], rows[HALF:]], axis=1).astype(jnp.bfloat16)
-            if e:
+                rows = velocity[(u * 4 + dz) * ROWS : (u * 4 + dz + 1) * ROWS]
+                gsrc[e, dz] = jnp.concatenate([rows[:HALF], rows[HALF:]], axis=1).astype(jnp.bfloat16)
+
+            @pl.when(e == 0)
+            def _():
+                gbuf[0] = gsrc[0]
+
+            @pl.when(e > 0)
+            def _():
                 pltpu.make_async_remote_copy(
                     src_ref=gsrc.at[e], dst_ref=gbuf.at[e], send_sem=sso, recv_sem=ro, device_id=peer_at(e), device_id_type=MESH
                 ).start()
 
-    arrived(qbuf, rq)
-    pass_on(0)
-
-    def chunk(g, _):
+    for g in range(EARLY):
+        pass_on(g)
+        if g == 2:
+            sent_chunk(2)
+            send_queries(2)
+    for g in range(EARLY):
         take(g)
-
-        @pl.when(g + AHEAD < CHUNKS)
-        def _():
-            send_chunk(g + AHEAD)
-
-        last = g == CHUNKS - 1
-        score(0, s_a)
-        for i in range(N_QB // 2):
-            if i == N_QB // 2 - 1:
-                pl.when(jnp.logical_not(last))(lambda: pass_on(g + 1))
-            score(2 * i + 1, s_b)
-            update(2 * i, s_a)
-            pl.when(last)(lambda: give_back(2 * i))
-            if i < N_QB // 2 - 1:
-                score(2 * i + 2, s_a)
-            update(2 * i + 1, s_b)
-            pl.when(last)(lambda: give_back(2 * i + 1))
+    arrived(queries_of(qbuf, 0), rq.at[0])
+
+    n_steps = CHUNKS * N_QB
+    n_early = EARLY * N_QB
+
+    def place_of(t):
+        early = t < n_early
+        major, minor = lax.div(t, 4), lax.rem(t, 4)
+        return jnp.where(early, minor, major), jnp.where(early, major, minor)
+
+    def step(t, now, then):
+        g, j = place_of(t)
+        after = jnp.minimum(t + 1, n_steps - 1)
+        g_after, j_after = place_of(after)
+        starts = lax.rem(t, 4) == 0
+
+        @pl.when(t == 0)
+        def _():
+            sent_chunk(3)
+            send_queries(3)
+
+        @pl.when(jnp.logical_and(starts, jnp.logical_and(t > 0, t < n_early)))
+        def _():
+            sent_queries(j)
+            send_chunk(j + 3)
+
+        @pl.when(t == n_early)
+        def _():
+            sent_chunk(4)
+            send_chunk(7)
+
+        @pl.when(jnp.logical_and(lax.rem(t, 4) == 3, t + 1 < n_early))
+        def _():
+            arrived(queries_of(qbuf, j_after), rq.at[j_after])
+
+        @pl.when(jnp.logical_and(lax.rem(t, 4) == 3, jnp.logical_and(t + 1 >= n_early, t + 1 < n_steps)))
+        def _():
+            take(g_after)
+
+        score(g_after, j_after, then)
+        update(g, j, now)
+
+        @pl.when(t >= n_steps - N_QB)
+        def _():
+            give_back(j)
+
+        @pl.when(jnp.logical_or(t == n_early - 2, jnp.logical_and(lax.rem(t, 4) == 1, jnp.logical_and(t > n_early, t < n_steps - 4))))
+        def _():
+            pass_on(lax.div(t + 3, 4))
+
+    score(0, 0, s_a)
+
+    def two_steps(n, _):
+        step(2 * n, s_a, s_b)
+        step(2 * n + 1, s_b, s_a)
         return 0
 
-    lax.fori_loop(0, CHUNKS, chunk, 0)
+    lax.fori_loop(0, n_steps // 2, two_steps, 0)
 
     arrived(gbuf.at[pl.ds(1, PEERS - 1)], ro)
     hsrc[...] = jnp.sum(gbuf[...].astype(jnp.float32), axis=0).astype(jnp.bfloat16)
@@ -369,7 +438,8 @@
                 for n in range(CH // 128):
                     dec_ref[r, f, y, :, pl.ds(n * 128, 128)] = dec_s[r, f, y, n].astype(jnp.bfloat16)
 
-    arrived(kvsrc, sskv)
+    for g in range(5, CHUNKS):
+        sent_chunk(g)
     arrived(gsrc.at[pl.ds(1, PEERS - 1)], sso)
     arrived(hsrc, ssh)
     arrived(xrecv.at[pl.ds(0, 3 * SEC - 1)], ssx)
@@ -381,12 +451,9 @@
     lax.fori_loop(0, CHUNKS, sent, 0)
 
 
-def hand_on(lat_ref, dec_ref, lat_out, dec_out, sems):
-    copies = [pltpu.make_async_copy(lat_ref, lat_out, sems.at[0]), pltpu.make_async_copy(dec_ref, dec_out, sems.at[1])]
-    for copy in copies:
-        copy.start()
-    for copy in copies:
-        copy.wait()
+def hand_on(lat_ref, dec_ref, lat_out, dec_out):
+    lat_out[...] = lat_ref[...]
+    dec_out[...] = dec_ref[...]
 
 
 def shards(
@@ -413,8 +480,8 @@
             pltpu.VMEM((STEPS, ROWS, HEAD_DIM), bf16),
             pltpu.VMEM((STEPS, KV_ROWS, HEAD_DIM), bf16),
             pltpu.VMEM((STEPS, KV_ROWS, HEAD_DIM), bf16),
-            pltpu.VMEM((KC, HEAD_DIM), bf16),
-            pltpu.VMEM((64, KC), bf16),
+            pltpu.VMEM((CHUNKS, KC, HEAD_DIM), bf16),
+            pltpu.VMEM((CHUNKS, 64, KC), bf16),
             pltpu.VMEM((N_QB, 64, QB), f32),
             pltpu.VMEM((N_QB, 8, QB), f32),
             pltpu.VMEM((N_QB, 8, QB), f32),
@@ -432,7 +499,7 @@
             pltpu.VMEM((768, 4 * CH), bf16),
             pltpu.VMEM((8 * RC, CH), f32),
             pltpu.VMEM((SEC, 2, 2, CH // 128, 2 * PCOLS, 128), f32),
-            dma, dma, dma((CHUNKS,)), dma, dma, dma, dma, dma((CHUNKS,)), dma((CHUNKS,)), dma, dma, dma, dma((8,)),
+            dma((N_QB,)), dma((CHUNKS,)), dma((CHUNKS,)), dma, dma, dma, dma((N_QB,)), dma((CHUNKS,)), dma((CHUNKS,)), dma, dma, dma, dma((8,)),
         ],
         compiler_params=pltpu.CompilerParams(collective_id=0, has_side_effects=True, vmem_limit_bytes=56 * 2**20),
         name="step",
@@ -454,9 +521,8 @@
     latents, decoded = pl.pallas_call(
         hand_on,
         out_shape=(jax.ShapeDtypeStruct(latents.shape, f32), jax.ShapeDtypeStruct(decoded.shape, bf16)),
-        in_specs=[pl.BlockSpec(memory_space=pltpu.HBM)] * 2,
-        out_specs=(anywhere, anywhere),
-        scratch_shapes=[dma((2,))],
+        in_specs=[vmem] * 2,
+        out_specs=(vmem, vmem),
         name="hand_on",
     )(latents, decoded)
     return latents.T[None], decoded

time: 108 us -> 100 us (0.926)
  Pallas kernels: 107 us -> 99.5 us
    pallas_call x1, Pallas kernels: 11 us -> 1.73 us  [shards(): pl.pallas_call(hand_on, out_shape=(jax.ShapeDtypeStruct(latents.shape, f3...]
    pallas_call x1, Pallas kernels: 96.1 us -> 97.7 us  [shards(): pl.pallas_call(kernel, out_shape=(jax.ShapeDtypeStruct((64, ROWS), f32),...]
where the time goes in v5:
time: 100 us
  Pallas kernels  99.5 us (100%)
    pallas_call x1, Pallas kernels, shards(): pl.pallas_call(kernel, out_shape=(jax.ShapeDtypeStruct((64, ROWS), f32),...  97.7 us

profile of v5, /device:TPU:1, one launch (start us, length us, event | category | flops | bytes accessed | tf_op | source)
XLA Modules:
  0.0 100.1 jit_solution(5187511404003589482)
XLA Ops:
  0.6 97.7 %step.1 = (f32[64,96]{1,0:T(8,128)}, bf16[4,2,2,24,384]{4,3,2,1,0:T(8,128)(2,1)}) custom-call(bf16[96,4096]{1,0:T(8,128)(2,1)} %bitcast.15, bf16[96,4096]{1,0:T(8,128)(2,1)} %bitcast.16, bf16[96,4096]{1,0:T(8,128)(2,1)} %bitcast.17, f32[1,4096]{1,0:T(1,128)} %bitcast.21, f32[1,4096]{1,0:T(1,128)} %bitcast.22, f32[64,96]{1,0:T(8,128)} %bitcast.20, ...), custom_call_target="tpu_custom_call" | custom-call | tf_op jit(solution)/shard_map/step/pallas_call | solution.py:466
  98.4 1.7 %hand_on.1 = (f32[64,96]{1,0:T(8,128)}, bf16[4,2,2,24,384]{4,3,2,1,0:T(8,128)(2,1)}) custom-call(f32[64,96]{1,0:T(8,128)} %get-tuple-element.6.lat_ref, bf16[4,2,2,24,384]{4,3,2,1,0:T(8,128)(2,1)} %get-tuple-element.7.dec_ref), custom_call_target="tpu_custom_call" | custom-call | tf_op jit(solution)/shard_map/hand_on/pallas_call | solution.py:521

commit v6 on v5

--- a/solution.py
+++ b/solution.py
@@ -191,6 +191,7 @@
 
     send_chunk(0)
     send_chunk(1)
+    send_chunk(2)
     wbig[...] = jnp.zeros_like(wbig)
     local[4].wait()
     for a in range(3):
@@ -206,11 +207,11 @@
     l_s[...] = jnp.zeros_like(l_s)
     m_s[...] = jnp.full_like(m_s, -1e30)
     sent_queries(0)
-    send_chunk(2)
+    send_chunk(3)
     sent_chunk(0)
-    send_chunk(3)
+    send_queries(1)
     sent_chunk(1)
-    send_queries(1)
+    send_queries(2)
 
     def pass_on(g):
         arrived(chunk_of(kvbuf, g), rkv.at[g])
@@ -270,7 +271,7 @@
         pass_on(g)
         if g == 2:
             sent_chunk(2)
-            send_queries(2)
+            send_queries(3)
     for g in range(EARLY):
         take(g)
     arrived(queries_of(qbuf, 0), rq.at[0])
@@ -281,7 +282,7 @@
     def place_of(t):
         early = t < n_early
         major, minor = lax.div(t, 4), lax.rem(t, 4)
-        return jnp.where(early, minor, major), jnp.where(early, major, minor)
+        return jnp.where(early, minor, major), jnp.where(early, major, lax.rem(2 * minor + 1, 5))
 
     def step(t, now, then):
         g, j = place_of(t)
@@ -292,17 +293,12 @@
         @pl.when(t == 0)
         def _():
             sent_chunk(3)
-            send_queries(3)
+            send_chunk(4)
 
         @pl.when(jnp.logical_and(starts, jnp.logical_and(t > 0, t < n_early)))
         def _():
             sent_queries(j)
-            send_chunk(j + 3)
-
-        @pl.when(t == n_early)
-        def _():
-            sent_chunk(4)
-            send_chunk(7)
+            send_chunk(j + 4)
 
         @pl.when(jnp.logical_and(lax.rem(t, 4) == 3, t + 1 < n_early))
         def _():
@@ -438,7 +434,7 @@
                 for n in range(CH // 128):
                     dec_ref[r, f, y, :, pl.ds(n * 128, 128)] = dec_s[r, f, y, n].astype(jnp.bfloat16)
 
-    for g in range(5, CHUNKS):
+    for g in range(4, CHUNKS):
         sent_chunk(g)
     arrived(gsrc.at[pl.ds(1, PEERS - 1)], sso)
     arrived(hsrc, ssh)

time: 100 us -> 99 us (0.990)
  Pallas kernels: 99.5 us -> 98.2 us
    pallas_call x1, Pallas kernels: 97.7 us -> 96.5 us  [shards(): pl.pallas_call(kernel, out_shape=(jax.ShapeDtypeStruct((64, ROWS), f32),...]
where the time goes in v6:
time: 99 us; the launch traced here: 98.8 us
  Pallas kernels  98.2 us (99%)
    pallas_call x1, Pallas kernels, shards(): pl.pallas_call(kernel, out_shape=(jax.ShapeDtypeStruct((64, ROWS), f32),...  96.5 us

profile of v6, /device:TPU:1, one launch (start us, length us, event | category | flops | bytes accessed | tf_op | source)
XLA Modules:
  0.0 98.8 jit_solution(9255314346391875604)
XLA Ops:
  0.6 96.5 %step.1 = (f32[64,96]{1,0:T(8,128)}, bf16[4,2,2,24,384]{4,3,2,1,0:T(8,128)(2,1)}) custom-call(bf16[96,4096]{1,0:T(8,128)(2,1)} %bitcast.15, bf16[96,4096]{1,0:T(8,128)(2,1)} %bitcast.16, bf16[96,4096]{1,0:T(8,128)(2,1)} %bitcast.17, f32[1,4096]{1,0:T(1,128)} %bitcast.21, f32[1,4096]{1,0:T(1,128)} %bitcast.22, f32[64,96]{1,0:T(8,128)} %bitcast.20, ...), custom_call_target="tpu_custom_call" | custom-call | tf_op jit(solution)/shard_map/step/pallas_call | solution.py:462
  97.1 1.7 %hand_on.1 = (f32[64,96]{1,0:T(8,128)}, bf16[4,2,2,24,384]{4,3,2,1,0:T(8,128)(2,1)}) custom-call(f32[64,96]{1,0:T(8,128)} %get-tuple-element.6.lat_ref, bf16[4,2,2,24,384]{4,3,2,1,0:T(8,128)(2,1)} %get-tuple-element.7.dec_ref), custom_call_target="tpu_custom_call" | custom-call | tf_op jit(solution)/shard_map/hand_on/pallas_call | solution.py:517

commit v7 on v6

--- a/solution.py
+++ b/solution.py
@@ -191,7 +191,6 @@
 
     send_chunk(0)
     send_chunk(1)
-    send_chunk(2)
     wbig[...] = jnp.zeros_like(wbig)
     local[4].wait()
     for a in range(3):
@@ -206,12 +205,6 @@
     acc[...] = jnp.zeros_like(acc)
     l_s[...] = jnp.zeros_like(l_s)
     m_s[...] = jnp.full_like(m_s, -1e30)
-    sent_queries(0)
-    send_chunk(3)
-    sent_chunk(0)
-    send_queries(1)
-    sent_chunk(1)
-    send_queries(2)
 
     def pass_on(g):
         arrived(chunk_of(kvbuf, g), rkv.at[g])
@@ -267,14 +260,16 @@
                     src_ref=gsrc.at[e], dst_ref=gbuf.at[e], send_sem=sso, recv_sem=ro, device_id=peer_at(e), device_id_type=MESH
                 ).start()
 
+    arrived(queries_of(qbuf, 0), rq.at[0])
+    send_chunk(2)
     for g in range(EARLY):
         pass_on(g)
-        if g == 2:
-            sent_chunk(2)
-            send_queries(3)
+        if g == 0:
+            send_chunk(3)
+        else:
+            send_queries(g)
     for g in range(EARLY):
         take(g)
-    arrived(queries_of(qbuf, 0), rq.at[0])
 
     n_steps = CHUNKS * N_QB
     n_early = EARLY * N_QB
@@ -288,22 +283,19 @@
         g, j = place_of(t)
         after = jnp.minimum(t + 1, n_steps - 1)
         g_after, j_after = place_of(after)
-        starts = lax.rem(t, 4) == 0
-
-        @pl.when(t == 0)
-        def _():
-            sent_chunk(3)
-            send_chunk(4)
-
-        @pl.when(jnp.logical_and(starts, jnp.logical_and(t > 0, t < n_early)))
-        def _():
-            sent_queries(j)
-            send_chunk(j + 4)
 
         @pl.when(jnp.logical_and(lax.rem(t, 4) == 3, t + 1 < n_early))
         def _():
             arrived(queries_of(qbuf, j_after), rq.at[j_after])
 
+            @pl.when(t == 3)
+            def _():
+                send_chunk(4)
+
+            @pl.when(t == n_early - 5)
+            def _():
+                send_chunk(5)
+
         @pl.when(jnp.logical_and(lax.rem(t, 4) == 3, jnp.logical_and(t + 1 >= n_early, t + 1 < n_steps)))
         def _():
             take(g_after)
@@ -318,6 +310,10 @@
         @pl.when(jnp.logical_or(t == n_early - 2, jnp.logical_and(lax.rem(t, 4) == 1, jnp.logical_and(t > n_early, t < n_steps - 4))))
         def _():
             pass_on(lax.div(t + 3, 4))
+
+            @pl.when(t < n_early + 4)
+            def _():
+                send_chunk(lax.div(t + 3, 4) + 2)
 
     score(0, 0, s_a)
 
@@ -434,7 +430,9 @@
                 for n in range(CH // 128):
                     dec_ref[r, f, y, :, pl.ds(n * 128, 128)] = dec_s[r, f, y, n].astype(jnp.bfloat16)
 
-    for g in range(4, CHUNKS):
+    for j in range(N_QB):
+        sent_queries(j)
+    for g in range(CHUNKS):
         sent_chunk(g)
     arrived(gsrc.at[pl.ds(1, PEERS - 1)], sso)
     arrived(hsrc, ssh)

time: 99 us -> 105 us (1.061)
  Pallas kernels: 98.2 us -> 104 us
    pallas_call x1, Pallas kernels: 96.5 us -> 102 us  [shards(): pl.pallas_call(kernel, out_shape=(jax.ShapeDtypeStruct((64, ROWS), f32),...]
where the time goes in v7:
time: 105 us; the launch traced here: 104 us
  Pallas kernels  104 us (99%)
    pallas_call x1, Pallas kernels, shards(): pl.pallas_call(kernel, out_shape=(jax.ShapeDtypeStruct((64, ROWS), f32),...  102 us

profile of v7, /device:TPU:1, one launch (start us, length us, event | category | flops | bytes accessed | tf_op | source)
XLA Modules:
  0.0 104.5 jit_solution(4338923855827297372)
XLA Ops:
  0.6 102.1 %step.1 = (f32[64,96]{1,0:T(8,128)}, bf16[4,2,2,24,384]{4,3,2,1,0:T(8,128)(2,1)}) custom-call(bf16[96,4096]{1,0:T(8,128)(2,1)} %bitcast.15, bf16[96,4096]{1,0:T(8,128)(2,1)} %bitcast.16, bf16[96,4096]{1,0:T(8,128)(2,1)} %bitcast.17, f32[1,4096]{1,0:T(1,128)} %bitcast.21, f32[1,4096]{1,0:T(1,128)} %bitcast.22, f32[64,96]{1,0:T(8,128)} %bitcast.20, ...), custom_call_target="tpu_custom_call" | custom-call | tf_op jit(solution)/shard_map/step/pallas_call | solution.py:460
  102.7 1.7 %hand_on.1 = (f32[64,96]{1,0:T(8,128)}, bf16[4,2,2,24,384]{4,3,2,1,0:T(8,128)(2,1)}) custom-call(f32[64,96]{1,0:T(8,128)} %get-tuple-element.6.lat_ref, bf16[4,2,2,24,384]{4,3,2,1,0:T(8,128)(2,1)} %get-tuple-element.7.dec_ref), custom_call_target="tpu_custom_call" | custom-call | tf_op jit(solution)/shard_map/hand_on/pallas_call | solution.py:515

commit v8 on v6

--- a/solution.py
+++ b/solution.py
@@ -192,6 +192,7 @@
     send_chunk(0)
     send_chunk(1)
     send_chunk(2)
+    send_chunk(3)
     wbig[...] = jnp.zeros_like(wbig)
     local[4].wait()
     for a in range(3):
@@ -207,9 +208,8 @@
     l_s[...] = jnp.zeros_like(l_s)
     m_s[...] = jnp.full_like(m_s, -1e30)
     sent_queries(0)
-    send_chunk(3)
+    send_queries(1)
     sent_chunk(0)
-    send_queries(1)
     sent_chunk(1)
     send_queries(2)
 

time: 99 us -> 99 us (level)
  no operation moved by 1% of the time
where the time goes in v8:
time: 99 us; the launch traced here: 98.8 us
  Pallas kernels  98.2 us (99%)
    pallas_call x1, Pallas kernels, shards(): pl.pallas_call(kernel, out_shape=(jax.ShapeDtypeStruct((64, ROWS), f32),...  96.5 us

profile of v8, /device:TPU:1, one launch (start us, length us, event | category | flops | bytes accessed | tf_op | source)
XLA Modules:
  0.0 98.8 jit_solution(9973232086812794014)
XLA Ops:
  0.6 96.5 %step.1 = (f32[64,96]{1,0:T(8,128)}, bf16[4,2,2,24,384]{4,3,2,1,0:T(8,128)(2,1)}) custom-call(bf16[96,4096]{1,0:T(8,128)(2,1)} %bitcast.15, bf16[96,4096]{1,0:T(8,128)(2,1)} %bitcast.16, bf16[96,4096]{1,0:T(8,128)(2,1)} %bitcast.17, f32[1,4096]{1,0:T(1,128)} %bitcast.21, f32[1,4096]{1,0:T(1,128)} %bitcast.22, f32[64,96]{1,0:T(8,128)} %bitcast.20, ...), custom_call_target="tpu_custom_call" | custom-call | tf_op jit(solution)/shard_map/step/pallas_call | solution.py:462
  97.1 1.7 %hand_on.1 = (f32[64,96]{1,0:T(8,128)}, bf16[4,2,2,24,384]{4,3,2,1,0:T(8,128)(2,1)}) custom-call(f32[64,96]{1,0:T(8,128)} %get-tuple-element.6.lat_ref, bf16[4,2,2,24,384]{4,3,2,1,0:T(8,128)(2,1)} %get-tuple-element.7.dec_ref), custom_call_target="tpu_custom_call" | custom-call | tf_op jit(solution)/shard_map/hand_on/pallas_call | solution.py:517
